TPU v7x, 32 devices: a whole 2x2x4 slice. The times are simulated.
32 devices in a mesh: frame: 2 (over x), pix: 16 (over z, y, core).
Axes of the slice: x: 2, y: 2, z: 4, core: 2. Of those that a mesh axis runs over, the one named last changes fastest.
Arguments:
- features: bfloat16 [2, 73728, 128], P('frame', 'pix'), may hold values from -6 to 6
- cotangent: bfloat16 [2, 73728, 128], P('frame', 'pix'), may hold values from -6 to 6
- slot_pair: int32 [16], P('pix'), may hold values from 0 to 15, each once
- crop_size: int32 [16, 2], replicated, may hold values from 40 to 112, as said below
- self_query: bfloat16 [128, 128], replicated, may hold values from -0.75 to 0.75
- self_key: bfloat16 [128, 128], replicated, may hold values from -0.5 to 0.5
- self_value: bfloat16 [128, 128], replicated, may hold values from -0.5 to 0.5
- self_merge: bfloat16 [128, 128], replicated, may hold values from -0.5 to 0.5
- self_gain: float32 [128], replicated, may hold values from 0.25 to 1.75
- self_bias: float32 [128], replicated, may hold values from -3 to 3
- cross_query: bfloat16 [128, 128], replicated, may hold values from -0.5 to 0.5
- cross_key: bfloat16 [128, 128], replicated, may hold values from -0.5 to 0.5
- cross_value: bfloat16 [128, 128], replicated, may hold values from -0.5 to 0.5
- cross_merge: bfloat16 [128, 128], replicated, may hold values from -0.5 to 0.5
- cross_gain: float32 [128], replicated, may hold values from 0.25 to 1.75
- cross_bias: float32 [128], replicated, may hold values from -3 to 3
- expand_weight: bfloat16 [256, 1024], replicated, may hold values from -0.375 to 0.375
- shrink_weight: bfloat16 [1024, 128], replicated, may hold values from -0.1875 to 0.1875
- final_gain: float32 [128], replicated, may hold values from 0.25 to 1.75
- final_bias: float32 [128], replicated, may hold values from -3 to 3
Outputs:
- features_out: bfloat16 [2, 73728, 128], P('frame', 'pix')
- input_grad: float32 [2, 73728, 128], P('frame', 'pix')
- grad_self_query: float32 [128, 128], replicated
- grad_self_key: float32 [128, 128], replicated
- grad_self_value: float32 [128, 128], replicated
- grad_self_merge: float32 [128, 128], replicated
- grad_self_gain: float32 [128], replicated
- grad_self_bias: float32 [128], replicated
- grad_cross_query: float32 [128, 128], replicated
- grad_cross_key: float32 [128, 128], replicated
- grad_cross_value: float32 [128, 128], replicated
- grad_cross_merge: float32 [128, 128], replicated
- grad_cross_gain: float32 [128], replicated
- grad_cross_bias: float32 [128], replicated
- grad_expand: float32 [256, 1024], replicated
- grad_shrink: float32 [1024, 128], replicated
- grad_final_gain: float32 [128], replicated
- grad_final_bias: float32 [128], replicated
Inputs may be any that keep to these rules, and one draw needn't show every extreme that they name: `slot_pair`: each pair is held by exactly one slot; pix index i holds slot i. `crop_size`: row p is the feature height and width of pair p: (46, 62) for half of the pairs and (40, 112) for the other half.
All inputs are finite; a program needn't handle non-finite values.
Results may differ from a plain program's by a relative error of at most 0.019.
The roundings to bfloat16 on the way count: a program that leaves them out, or rounds other values in their place, can miss the bound.
Values may be sent and summed in bfloat16 or wider, within the bound.
A program may use at most 192 MiB of HBM per device.

v0:
```python
import functools
import math
import types

import jax
import jax.numpy as jnp
from jax import lax
from jax.experimental import pallas as pl
from jax.experimental.pallas import tpu as pltpu
from jax.sharding import PartitionSpec as P

WSLOT = 1152
FEWEST = 704
NEGATIVE = -1e30
EPSILON = 1e-05
LOG2E = 1.4426950408889634
F32 = jnp.float32
BF16 = jnp.bfloat16
MESH = pl.DeviceIdType.MESH
TAIL_SHIFT = 2.7777777777777777
TAIL_POLY = (0.39765776262463953, 1.1594294101832299, 1.9333185594349698, 10.032517622923805, -5.2492700447308085, -9.371923274701059)
SPAN = 256
CHUNK = 128
TILES = ((0, 256), (256, 256), (512, 256), (768, 256), (1024, 128))
ONES = 16


def nn(left, right):
    return jnp.dot(left, right, preferred_element_type=F32)


def nt(left, right):
    return lax.dot_general(left, right, (((1,), (1,)), ((), ())), preferred_element_type=F32)


def norm_stats(values):
    centre = jnp.mean(values, axis=0, keepdims=True)
    shifted = values - centre
    spread = jnp.mean(shifted * shifted, axis=0, keepdims=True)
    inverse = lax.rsqrt(spread + EPSILON)
    return shifted * inverse, inverse


def norm_back(hat, inverse, gain, upstream):
    scaled = upstream * gain
    first = jnp.mean(scaled, axis=0, keepdims=True)
    second = jnp.mean(scaled * hat, axis=0, keepdims=True)
    return inverse * (scaled - first - hat * second)


def gelu_both(values):
    bell = jnp.exp2(values * (values * (-0.5 * LOG2E))).astype(BF16)
    t = (1.0 / (jnp.abs(values) + TAIL_SHIFT)).astype(BF16)
    low = values.astype(BF16)
    poly = t * BF16(TAIL_POLY[-1]) + BF16(TAIL_POLY[-2])
    for coefficient in TAIL_POLY[-3::-1]:
        poly = poly * t + BF16(coefficient)
    tail = poly * t * bell
    phi = jnp.where(low >= BF16(0.0), BF16(1.0) - tail, tail)
    return low * phi, phi + low * bell * BF16(1.0 / math.sqrt(2.0 * math.pi))


def flip(values):
    return values.astype(F32).T.astype(BF16)


INPUTS = (
    "x", "cot", "slot", "crop", "sq", "sk", "sv", "sm", "sgain", "sbias",
    "cq", "ck", "cv", "cm", "cgain", "cbias", "we", "ws", "fgain", "fbias",
)
OUTPUTS = ("result", "grad", "feed_out", "cross_out", "self_out", "totals")
VECTORS = ("sgain", "sbias", "cgain", "cbias", "fgain", "fbias")


def layer_kernel(sizes, *refs):
    names = INPUTS + OUTPUTS + tuple(scratch_shapes(sizes))
    r = types.SimpleNamespace(**dict(zip(names, refs, strict=True)))
    width, hidden, windows, peers = sizes.width, sizes.hidden, sizes.windows, sizes.peers
    factor = 1.0 / math.sqrt(width)
    scale = factor * LOG2E
    frame = lax.axis_index("frame")
    pix = lax.axis_index("pix")
    core = lax.rem(pix, 2)
    me = frame * (peers // 2) + lax.div(pix, 2)
    partner = (1 - frame, pix)
    sibling = (frame, pix + 1 - 2 * core)

    def peer(step):
        index = lax.rem(me + step, peers)
        return index, (lax.div(index, peers // 2), lax.rem(index, peers // 2) * 2 + core)

    barrier = pltpu.get_barrier_semaphore()
    pl.semaphore_signal(barrier, inc=1, device_id=sibling, device_id_type=MESH)

    def greet(step, carry):
        pl.semaphore_signal(barrier, inc=1, device_id=peer(step)[1], device_id_type=MESH)
        return carry

    lax.fori_loop(1, peers, greet, 0)

    slot = r.slot[0]
    live = lax.shift_right_logical(r.crop[0, slot], 1) * lax.shift_right_logical(r.crop[1, slot], 1)

    r.eye[...] = jnp.where(
        lax.broadcasted_iota(jnp.int32, (width, width), 0)
        == lax.broadcasted_iota(jnp.int32, (width, width), 1),
        1.0, 0.0,
    ).astype(BF16)
    r.self_qv_t[:width] = flip(r.sq[...])
    r.self_qv_t[width:] = flip(r.sv[...])
    r.self_k_t[...] = flip(r.sk[...])
    r.self_merge_t[...] = flip(r.sm[...])
    r.self_qkv[:, :width] = r.sq[...]
    r.self_qkv[:, width : 2 * width] = r.sk[...]
    r.self_qkv[:, 2 * width :] = r.sv[...]
    for i, name in enumerate(VECTORS):
        r.vectors[i] = jnp.broadcast_to(getattr(r, name)[...], (width, CHUNK)).T
    vector = lambda name: r.vectors[VECTORS.index(name)]
    for name in ("g_sqkv", "g_sm", "g_cqkv", "g_cm", "g_we", "g_ws", "g_vec"):
        getattr(r, name)[...] = jnp.zeros_like(getattr(r, name))
    r.v_aug[width:, :] = jnp.ones((ONES, WSLOT), BF16)

    def alive_at(start, size):
        token = lax.broadcasted_iota(jnp.int32, (1, size), 1) + lax.rem(start, WSLOT)
        return jnp.where(token < live, 1.0, 0.0)

    def rows_at(w):
        return pl.ds(pl.multiple_of(w * WSLOT, WSLOT), WSLOT)

    def cols_at(w, start=0, size=WSLOT):
        return pl.ds(pl.multiple_of(w * WSLOT + start, 128), size)

    def send_rows(w):
        return pltpu.make_async_remote_copy(
            src_ref=r.send.at[rows_at(w), :], dst_ref=r.other.at[rows_at(w), :],
            send_sem=r.sem_x.at[0, w], recv_sem=r.sem_x.at[1, w], device_id=partner, device_id_type=MESH,
        )

    def send_back(w):
        return pltpu.make_async_remote_copy(
            src_ref=r.back.at[w], dst_ref=r.received.at[w],
            send_sem=r.sem_b.at[0, w], recv_sem=r.sem_b.at[1, w], device_id=partner, device_id_type=MESH,
        )

    def store_rows(target, stage, w, sem, back=None):
        place = w if back is None else lax.rem(w, 2)
        w = w if back is None else w + back
        return pltpu.make_async_copy(stage.at[rows_at(place), :], target.at[rows_at(w), :], sem.at[w])

    def attend(w, exps, out, inverse):
        bufs = (r.buf_a, r.buf_b)

        def score(t):
            first, size = TILES[t]
            got = nn(r.k[...], r.q_t[:, cols_at(w, first, size)])
            rest = got[FEWEST:]
            row = lax.broadcasted_iota(jnp.int32, rest.shape, 0) + FEWEST
            rest = jnp.where(row < live, rest, NEGATIVE)
            bufs[t % 2][:FEWEST, :size] = got[:FEWEST]
            bufs[t % 2][FEWEST:, :size] = rest
            return scale * jnp.maximum(
                jnp.max(got[:FEWEST], axis=0, keepdims=True), jnp.max(rest, axis=0, keepdims=True)
            )

        def output_part(t, rows, total):
            first, size = TILES[t]
            part = nn(r.v_aug[:, rows], exps[w, rows, first : first + size])
            return part if total is None else total + part

        def output(t, both):
            first, size = TILES[t]
            share = 1.0 / both[width : width + 1]
            inverse[:, cols_at(w, first, size)] = share
            out[:, cols_at(w, first, size)] = (both[:width] * share).astype(BF16)

        top = score(0)
        for t, (first, size) in enumerate(TILES):
            after = score(t + 1) if t + 1 < len(TILES) else None
            total = None
            for start, count in TILES:
                rows = slice(start, start + count)
                if t:
                    total = output_part(t - 1, rows, total)
                exps[w, rows, first : first + size] = jnp.exp2(
                    bufs[t % 2][rows, :size] * scale - top
                ).astype(BF16)
            if t:
                output(t - 1, total)
            top = after
        last = len(TILES) - 1
        output(last, output_part(last, slice(0, WSLOT), None))

    def attend_back(w, exps):
        def query(t):
            first, size = TILES[t]
            cols = slice(first, first + size)
            r.dqkv[:width, cols] = (nn(r.k_t[...], r.diff[:, cols]) * factor).astype(BF16)

        for t, (first, size) in enumerate(TILES):
            cols = slice(first, first + size)
            grad = nn(r.v[...], r.up[:, cols]) - r.inner[:, cols]
            r.diff[:, cols] = exps[w, :, cols] * grad.astype(BF16)
            if t:
                query(t - 1)
        grad_value = nt(exps[w], r.up[...])
        query(len(TILES) - 1)
        grad_key = nt(r.diff[...], r.q_t[:, cols_at(w)]) * factor
        r.dqkv[2 * width :, :] = grad_value.T.astype(BF16)
        r.dqkv[width : 2 * width, :] = grad_key.T.astype(BF16)

    def forward_self(w, carry):
        x = r.x[rows_at(w), :]
        stacked = nt(r.self_qv_t[...], x).astype(BF16)
        r.q_t[:, cols_at(w)] = stacked[:width]
        r.v_aug[:width, :] = stacked[width:]
        r.k[...] = nn(x, r.sk[...]).astype(BF16)
        attend(w, r.exps, r.out_one, r.inverse_one)
        merged = nn(r.self_merge_t[...], r.out_one[:, cols_at(w)])
        x_t = nt(r.eye[...], r.x[rows_at(w), :])
        for start in range(0, WSLOT, CHUNK):
            cols = slice(start, start + CHUNK)
            hat, _ = norm_stats(merged[:, cols])
            x1 = x_t[:, cols] + hat * vector("sgain") + vector("sbias")
            r.x1[:, cols_at(w, start, CHUNK)] = x1
            r.concat[:width, cols_at(w, start, CHUNK)] = x1.astype(BF16)
            r.send[pl.ds(pl.multiple_of(w * WSLOT + start, CHUNK), CHUNK), :] = x1.T.astype(BF16)

        @pl.when(w == 0)
        def _():
            pl.semaphore_wait(barrier, peers)

        send_rows(w).start()
        return carry

    lax.fori_loop(0, windows, forward_self, 0)

    r.cross_q_t[...] = flip(r.cq[...])
    r.cross_k_t[...] = flip(r.ck[...])
    r.cross_v_t[...] = flip(r.cv[...])
    r.cross_merge_t[...] = flip(r.cm[...])
    r.cross_kv[:, :width] = r.ck[...]
    r.cross_kv[:, width:] = r.cv[...]
    r.expand_t[...] = flip(r.we[...])
    r.shrink_t[...] = flip(r.ws[...])

    def forward_cross(w, carry):
        r.q_t[:, cols_at(w)] = nn(r.cross_q_t[...], r.concat[:width, cols_at(w)]).astype(BF16)
        send_rows(w).wait()
        other = r.other[rows_at(w), :]
        r.v_aug[:width, :] = nt(r.cross_v_t[...], other).astype(BF16)
        r.k[...] = nn(other, r.ck[...]).astype(BF16)
        attend(w, r.exps_two, r.out_two, r.inverse_two)
        merged = nn(r.cross_merge_t[...], r.out_two[:, cols_at(w)])
        for start in range(0, WSLOT, CHUNK):
            hat, _ = norm_stats(merged[:, start : start + CHUNK])
            r.concat[width:, cols_at(w, start, CHUNK)] = (
                hat * vector("cgain") + vector("cbias")
            ).astype(BF16)
        return carry

    lax.fori_loop(0, windows, forward_cross, 0)

    spans = sizes.rows // SPAN

    def span(i):
        return pl.ds(pl.multiple_of(i * SPAN, SPAN), SPAN)

    def norm_tile(i, b, branch, up_all, start):
        part = slice(start, start + CHUNK)
        here = pl.ds(pl.multiple_of(i * SPAN + start, CHUNK), CHUNK)
        alive = alive_at(i * SPAN + start, CHUNK)
        hat, inverse = norm_stats(branch[:, part])
        result = (r.x1[:, here] + hat * vector("fgain") + vector("fbias")) * alive
        r.result_stage[here, :] = result.T.astype(BF16)
        up = up_all[:, part] * alive
        r.x1[:, here] = up
        r.g_vec[4] += up * hat
        r.g_vec[5] += up
        r.branch[b, :, part] = norm_back(hat, inverse, vector("fgain"), up).astype(BF16)

    def settle(i, total):
        r.x1[:, span(i)] += total[:width]
        r.grad_normed[:, span(i)] = total[width:]

    parts = [slice(start, start + SPAN) for start in range(0, hidden, SPAN)]

    def expand(i):
        r.buf_a[:hidden, :] = nn(r.expand_t[...], r.concat[:, span(i)])

    def activate(b, rows):
        act, slope = gelu_both(r.buf_a[rows, :])
        r.act[b, rows, :] = act
        r.slope[b, rows, :] = slope

    def hide(b):
        r.hid[...] = r.slope[b] * nn(r.ws[...], r.branch[b]).astype(BF16)

    def add(total, part):
        return part if total is None else total + part

    for name in ("act", "slope", "branch"):
        getattr(r, name)[2] = jnp.zeros(getattr(r, name).shape[1:], BF16)
    expand(0)
    for rows in parts:
        activate(0, rows)

    def feed(j, carry):
        for b in range(3):
            i = 3 * j + b
            old = (b + 2) % 3
            before = jnp.maximum(i - 1, 0)
            expand(jnp.minimum(i + 1, spans - 1))
            hide(old)
            branch, total = None, None
            for rows in parts:
                branch = add(branch, nn(r.shrink_t[:, rows], r.act[b, rows, :]))
                total = add(total, nn(r.we[:, rows], r.hid[rows, :]))
                activate((b + 1) % 3, rows)
            settle(before, total)
            up_all = nt(r.eye[...], r.cot[span(i), :])
            for_shrink = nt(r.act[old], r.branch[old])
            norm_tile(i, b, branch, up_all, 0)
            for_expand = nt(r.hid[...], r.concat[:, span(before)])
            norm_tile(i, b, branch, up_all, CHUNK)
            r.g_ws[...] += for_shrink
            r.g_we[...] += for_expand
        return carry

    lax.fori_loop(0, spans // 3, feed, 0)
    last = (spans - 1) % 3
    hide(last)
    settle(spans - 1, nn(r.we[...], r.hid[...]))
    r.g_ws[...] += nt(r.act[last], r.branch[last])
    r.g_we[...] += nt(r.hid[...], r.concat[:, span(spans - 1)])

    def store_result(w, carry):
        store_rows(r.result, r.result_stage, w, r.sem_result).start()
        return carry

    lax.fori_loop(0, windows, store_result, 0)

    feed_sum = Reduction(r, sizes.plans["feed"], "feed", sizes.scale, sibling, peer, core, me)
    cross_sum = Reduction(r, sizes.plans["cross"], "cross", sizes.scale, sibling, peer, core, me)
    self_sum = Reduction(r, sizes.plans["self"], "self", sizes.scale, sibling, peer, core, me)
    feed_sum.begin([r.g_we.at[:, pl.ds(0, width)], r.g_we.at[:, pl.ds(width, width)], r.g_ws])

    def upstream(w, merged, grad_at, number, gain, out, gradient, merge, inverse):
        sums = [jnp.zeros((width, CHUNK), F32)] * 2
        for start in range(0, WSLOT, CHUNK):
            hat, root = norm_stats(merged[:, start : start + CHUNK])
            grad = grad_at(start)
            sums = [sums[0] + grad * hat, sums[1] + grad]
            r.grad_merged[:, start : start + CHUNK] = norm_back(hat, root, vector(gain), grad).astype(BF16)
        r.g_vec[number] += sums[0]
        r.g_vec[number + 1] += sums[1]
        out = out[:, cols_at(w)]
        gradient[...] += nt(out, r.grad_merged[...])
        up = (nn(merge[...], r.grad_merged[...]) * inverse[:, cols_at(w)]).astype(BF16)
        r.up[...] = up
        r.inner[...] = jnp.sum(up.astype(F32) * out.astype(F32), axis=0, keepdims=True)

    def backward_cross(w, carry):
        @pl.when(w == 1)
        def _():
            feed_sum.scatter()

        @pl.when(w == windows - 1)
        def _():
            feed_sum.gather()

        upstream(
            w, nn(r.cross_merge_t[...], r.out_two[:, cols_at(w)]),
            lambda start: r.grad_normed[:, cols_at(w, start, CHUNK)],
            2, "cgain", r.out_two, r.g_cm, r.cm, r.inverse_two,
        )
        other = r.other[rows_at(w), :]
        r.k_t[...] = nt(r.cross_k_t[...], other).astype(BF16)
        r.v[...] = nn(other, r.cv[...]).astype(BF16)
        attend_back(w, r.exps_two)
        r.back[w] = nn(r.cross_kv[...], r.dqkv[width:, :]).astype(BF16)
        send_back(w).start()
        r.g_cqkv[:width] += nt(r.dqkv[:width, :], r.concat[:width, cols_at(w)])
        r.g_cqkv[width:] += nn(r.dqkv[width:, :], r.other[rows_at(w), :])
        r.x1[:, cols_at(w)] += nn(r.cq[...], r.dqkv[:width, :])
        return carry

    lax.fori_loop(0, windows, backward_cross, 0)
    cross_sum.begin([r.g_cqkv, r.g_cm])

    def backward_self(w, carry):
        @pl.when(w == 1)
        def _():
            feed_sum.share()
            cross_sum.scatter()

        @pl.when(w == windows - 1)
        def _():
            feed_sum.finish()
            feed_sum.store(r.feed_out).start()
            cross_sum.gather()

        x = r.x[rows_at(w), :]
        r.q_t[:, cols_at(w)] = nt(r.self_qv_t[:width, :], x).astype(BF16)
        r.k_t[...] = nt(r.self_k_t[...], x).astype(BF16)
        r.v[...] = nn(x, r.sv[...]).astype(BF16)
        send_back(w).wait()

        def grad_at(start):
            here = cols_at(w, start, CHUNK)
            grad = r.x1[:, here] + r.received[w, :, start : start + CHUNK].astype(F32)
            r.x1[:, here] = grad
            return grad

        upstream(
            w, nn(r.self_merge_t[...], r.out_one[:, cols_at(w)]), grad_at,
            0, "sgain", r.out_one, r.g_sm, r.sm, r.inverse_one,
        )
        attend_back(w, r.exps)
        r.g_sqkv[...] += nn(r.dqkv[...], r.x[rows_at(w), :])

        @pl.when(w >= 2)
        def _():
            store_rows(r.grad, r.grad_stage, w, r.sem_grad, -2).wait()

        total = r.x1[:, cols_at(w)] + nn(r.self_qkv[...], r.dqkv[...])
        r.grad_stage[pl.ds(pl.multiple_of(lax.rem(w, 2) * WSLOT, WSLOT), WSLOT), :] = total.T
        store_rows(r.grad, r.grad_stage, w, r.sem_grad, 0).start()
        return carry

    lax.fori_loop(0, windows, backward_self, 0)
    self_sum.begin([r.g_sqkv, r.g_sm], r.g_vec)
    cross_sum.share()
    self_sum.scatter()
    cross_sum.finish()
    cross_sum.store(r.cross_out).start()
    self_sum.gather()
    if self_sum.full:
        r.totals[...] = self_sum.vector_total()
    self_sum.share()
    self_sum.finish()
    self_sum.store(r.self_out).start()
    if not self_sum.full:
        r.totals[...] = self_sum.total[0, 0, self_sum.shard :].astype(F32)

    def drain(w, carry):
        store_rows(r.result, r.result_stage, w, r.sem_result).wait()

        @pl.when(w >= windows - 2)
        def _():
            store_rows(r.grad, r.grad_stage, w, r.sem_grad, 0).wait()

        return carry

    lax.fori_loop(0, windows, drain, 0)
    feed_sum.store(r.feed_out).wait()
    cross_sum.store(r.cross_out).wait()
    self_sum.store(r.self_out).wait()


class Reduction:
    def __init__(self, r, plan, name, scale, sibling, peer, core, me):
        self.sibling, self.peer, self.core, self.me = sibling, peer, core, me
        self.scale = scale
        self.peers, self.owners, self.shard, self.extra, self.kept = (
            plan.peers, plan.owners, plan.shard, plan.extra, plan.kept
        )
        self.half = self.owners * self.shard
        self.full = self.owners == self.peers
        for field in ("pack", "from_sibling", "inbox", "total", "sems"):
            setattr(self, field, getattr(r, name + "_" + field))

    def copy(self, source, target, number, device):
        return pltpu.make_async_remote_copy(
            src_ref=source, dst_ref=target, send_sem=self.sems.at[0, number],
            recv_sem=self.sems.at[1, number], device_id=device, device_id_type=MESH,
        )

    def owning(self, then, otherwise=None):
        if self.full:
            then()
        else:
            pl.when(self.me < self.owners)(then)
            if otherwise is not None:
                pl.when(self.me >= self.owners)(otherwise)

    def halves(self):
        return self.copy(self.pack.at[1 - self.core], self.from_sibling, 0, self.sibling)

    def begin(self, pieces, vec=None):
        at = 0
        width = self.pack.shape[3]
        for piece in pieces:
            taken = 0
            while taken < piece.shape[0]:
                which, inside = divmod(at, self.half)
                index, offset = divmod(inside, self.shard)
                left = piece.shape[0] - taken
                if offset or left < self.shard:
                    count = min(left, self.shard - offset)
                    self.pack[which, index, offset : offset + count] = piece[
                        taken : taken + count, :
                    ].astype(BF16)
                else:
                    blocks = min(left // self.shard, self.owners - index)
                    count = blocks * self.shard
                    self.pack[which, index : index + blocks, : self.shard] = (
                        piece[taken : taken + count, :].astype(BF16).reshape(blocks, self.shard, width)
                    )
                at += count
                taken += count
        while at < 2 * self.half:
            which, inside = divmod(at, self.half)
            index, offset = divmod(inside, self.shard)
            count = self.shard - offset
            self.pack[which, index, offset : self.shard] = jnp.zeros((count, width), BF16)
            at += count
        if self.extra:
            sums = jnp.concatenate([jnp.sum(vec[i].T, axis=0, keepdims=True) for i in range(vec.shape[0])])
            rows = jnp.concatenate([sums, jnp.zeros((self.extra - vec.shape[0], width), F32)]).astype(BF16)
            for which in range(2):
                self.pack[which, :, self.shard :] = jnp.broadcast_to(
                    rows[None], (self.owners, self.extra, width)
                )
        self.halves().start()

    def wait(self, number, sent, received):
        if sent is not None:
            self.copy(sent, sent, number, self.sibling).wait_send()
        if received is not None:
            self.copy(received, received, number, self.sibling).wait_recv()

    def scatter(self):
        self.halves().wait()
        mine = self.pack[self.core].astype(F32) + self.from_sibling[...].astype(F32)
        self.pack[self.core] = mine.astype(BF16)

        def send(step, carry):
            index, device = self.peer(step)

            def go():
                place = self.pack.at[self.core, index]
                self.copy(place, self.inbox.at[self.me], 1, device).start()

            go() if self.full else pl.when(index < self.owners)(go)
            return carry

        lax.fori_loop(1, self.peers, send, 0)

        def own():
            self.inbox[self.me] = self.pack[self.core, self.me]

        self.owning(own)

    def gather(self):
        def own():
            self.wait(
                1, self.pack.at[0, pl.ds(0, self.owners - 1)], self.inbox.at[pl.ds(0, self.peers - 1)]
            )
            total = jnp.sum(self.inbox[:, : self.kept].astype(F32), axis=0) * self.scale
            self.total[self.core, self.me] = total.astype(BF16)

            def send(step, carry):
                place = self.total.at[self.core, self.me]
                self.copy(place, place, 2, self.peer(step)[1]).start()
                return carry

            lax.fori_loop(1, self.peers, send, 0)

        self.owning(own, lambda: self.wait(1, self.pack.at[0], None))

    def vector_total(self):
        return jnp.sum(self.inbox[:, self.shard :].astype(F32), axis=0) * self.scale

    def share(self):
        def own():
            for count in (self.owners - 1,) * ((self.peers - 1) // (self.owners - 1)) + (
                (self.peers - 1) % (self.owners - 1),
            ):
                if count:
                    self.wait(2, self.total.at[0, pl.ds(0, count)], None)
            self.wait(2, None, self.total.at[0, pl.ds(0, self.owners - 1)])

        self.owning(own, lambda: self.wait(2, None, self.total.at[0]))
        self.copy(self.total.at[self.core], self.total.at[self.core], 3, self.sibling).start()

    def finish(self):
        self.copy(self.total.at[self.core], self.total.at[self.core], 3, self.sibling).wait()

    def store(self, target):
        return pltpu.make_async_copy(self.total, target, self.sems.at[0, 4])


def scratch_shapes(sizes):
    width, hidden, windows, rows, peers = sizes.width, sizes.hidden, sizes.windows, sizes.rows, sizes.peers
    vmem = pltpu.VMEM
    dma = pltpu.SemaphoreType.DMA
    square = vmem((width, width), F32)
    shapes = {
        "eye": vmem((width, width), BF16),
        "self_qv_t": vmem((2 * width, width), BF16),
        "self_k_t": vmem((width, width), BF16),
        "self_merge_t": vmem((width, width), BF16),
        "self_qkv": vmem((width, 3 * width), BF16),
        "vectors": vmem((len(VECTORS), width, CHUNK), F32),
        "cross_q_t": vmem((width, width), BF16),
        "cross_k_t": vmem((width, width), BF16),
        "cross_v_t": vmem((width, width), BF16),
        "cross_merge_t": vmem((width, width), BF16),
        "cross_kv": vmem((width, 2 * width), BF16),
        "expand_t": vmem((hidden, 2 * width), BF16),
        "shrink_t": vmem((width, hidden), BF16),
        "g_sqkv": vmem((3 * width, width), F32),
        "g_cqkv": vmem((3 * width, width), F32),
        "g_sm": square,
        "g_cm": square,
        "g_we": vmem((hidden, 2 * width), F32),
        "g_ws": vmem((hidden, width), F32),
        "g_vec": vmem((len(VECTORS), width, CHUNK), F32),
        "q_t": vmem((width, rows), BF16),
        "k": vmem((WSLOT, width), BF16),
        "v_aug": vmem((width + ONES, WSLOT), BF16),
        "out_one": vmem((width, rows), BF16),
        "out_two": vmem((width, rows), BF16),
        "inverse_one": vmem((1, rows), F32),
        "inverse_two": vmem((1, rows), F32),
        "x1": vmem((width, rows), F32),
        "concat": vmem((2 * width, rows), BF16),
        "send": vmem((rows, width), BF16),
        "other": vmem((rows, width), BF16),
        "back": vmem((windows, width, WSLOT), BF16),
        "received": vmem((windows, width, WSLOT), BF16),
        "grad_normed": vmem((width, rows), F32),
        "exps": vmem((windows, WSLOT, WSLOT), BF16),
        "exps_two": vmem((windows, WSLOT, WSLOT), BF16),
        "diff": vmem((WSLOT, WSLOT), BF16),
        "act": vmem((3, hidden, SPAN), BF16),
        "slope": vmem((3, hidden, SPAN), BF16),
        "branch": vmem((3, width, SPAN), BF16),
        "hid": vmem((hidden, SPAN), BF16),
        "buf_a": vmem((max(WSLOT, hidden), SPAN), F32),
        "buf_b": vmem((WSLOT, SPAN), F32),
        "grad_merged": vmem((width, WSLOT), BF16),
        "k_t": vmem((width, WSLOT), BF16),
        "v": vmem((WSLOT, width), BF16),
        "up": vmem((width, WSLOT), BF16),
        "inner": vmem((1, WSLOT), F32),
        "dqkv": vmem((3 * width, WSLOT), BF16),
        "result_stage": vmem((rows, width), BF16),
        "grad_stage": vmem((2 * WSLOT, width), F32),
        "sem_x": dma((2, windows)),
        "sem_b": dma((2, windows)),
        "sem_result": dma((windows,)),
        "sem_grad": dma((windows,)),
    }
    for name, plan in sizes.plans.items():
        part = plan.shard + plan.extra
        shapes[name + "_pack"] = vmem((2, plan.owners, part, width), BF16)
        shapes[name + "_from_sibling"] = vmem((plan.owners, part, width), BF16)
        shapes[name + "_inbox"] = vmem((peers, part, width), BF16)
        shapes[name + "_total"] = vmem((2, plan.owners, plan.kept, width), BF16)
        shapes[name + "_sems"] = dma((2, 5))
    return shapes


def total_rows(total, shard, start, count):
    _, peers, _, width = total.shape
    at = start
    found = []
    while at < start + count:
        which, inside = divmod(at, peers * shard)
        index, offset = divmod(inside, shard)
        left = start + count - at
        if offset or left < shard:
            take = min(shard - offset, left)
            found.append(total[which, index, offset : offset + take])
        else:
            blocks = min(left // shard, peers - index)
            take = blocks * shard
            found.append(total[which, index : index + blocks, :shard].reshape(take, width))
        at += take
    return found[0] if len(found) == 1 else jnp.concatenate(found, axis=0)


def hand_out(sizes, *refs):
    result_in, grad_in, feed, cross, own, totals, result, grad = refs[:8]
    (o_sq, o_sk, o_sv, o_sm, o_sgain, o_sbias, o_cq, o_ck, o_cv, o_cm, o_cgain, o_cbias,
     o_we, o_ws, o_fgain, o_fbias) = refs[8:24]
    width, hidden = sizes.width, sizes.hidden
    shards = [plan.shard for plan in sizes.plans.values()]
    result[...] = result_in[...]
    grad[...] = grad_in[...]

    @pl.when(pl.program_id(0) == 0)
    def _():
        o_we[:width, :] = total_rows(feed, shards[0], 0, hidden).astype(F32).T
        o_we[width:, :] = total_rows(feed, shards[0], hidden, hidden).astype(F32).T
        o_ws[...] = total_rows(feed, shards[0], 2 * hidden, hidden).astype(F32)
        for source, shard, group in (
            (cross, shards[1], (o_cq, o_ck, o_cv, o_cm)), (own, shards[2], (o_sq, o_sk, o_sv, o_sm))
        ):
            for i, ref in enumerate(group):
                total = total_rows(source, shard, i * width, width).astype(F32)
                ref[...] = total if i == 3 else total.T
        for i, ref in enumerate((o_sgain, o_sbias, o_cgain, o_cbias, o_fgain, o_fbias)):
            ref[...] = totals[i : i + 1, :]


def local(features, cotangent, slot_pair, crop_size, *weights):
    rows, width = features.shape[1:]
    hidden = weights[12].shape[1]
    peers = lax.axis_size("pix")

    def plan(count, extra=0):
        shard = -(-count // (2 * peers * 16)) * 16
        owners = min(peers, -(-count // (2 * shard)))
        kept = shard + (extra if owners < peers else 0)
        return types.SimpleNamespace(peers=peers, owners=owners, shard=shard, extra=extra, kept=kept)

    sizes = types.SimpleNamespace(
        rows=rows, width=width, hidden=hidden, windows=rows // WSLOT, peers=peers,
        scale=1.0 / math.sqrt(2.0 * rows * peers),
        plans={"feed": plan(3 * hidden), "cross": plan(4 * width), "self": plan(4 * width, 16)},
    )
    flat = lambda value: value.reshape(1, -1) if value.ndim == 1 else value
    shape = jax.ShapeDtypeStruct
    small = pl.BlockSpec(memory_space=pltpu.VMEM)
    large = pl.BlockSpec(memory_space=pl.ANY)
    scalar = pl.BlockSpec(memory_space=pltpu.SMEM)
    square = shape((width, width), F32)
    row = shape((1, width), F32)
    big = [shape((rows, width), BF16), shape((rows, width), F32)]
    middle = pl.pallas_call(
        functools.partial(layer_kernel, sizes),
        in_specs=[small, small, scalar, scalar] + [small] * 16,
        out_specs=[large] * 5 + [small],
        out_shape=big + [
            shape((2, plan.owners, plan.kept, width), BF16) for plan in sizes.plans.values()
        ] + [shape((16, width), F32)],
        scratch_shapes=list(scratch_shapes(sizes).values()),
        compiler_params=pltpu.CompilerParams(
            collective_id=0, has_side_effects=True, vmem_limit_bytes=63 * 2**20
        ),
        name="layer",
    )(features[0], cotangent[0], slot_pair, crop_size.T, *[flat(weight) for weight in weights])
    moved = [pl.BlockSpec((WSLOT, width), lambda w: (w, 0))] * 2
    whole = lambda shape: pl.BlockSpec(shape, lambda w: (0,) * len(shape))
    smalls = [
        square, square, square, square, row, row, square, square, square, square, row, row,
        shape((2 * width, hidden), F32), shape((hidden, width), F32), row, row,
    ]
    outs = pl.pallas_call(
        functools.partial(hand_out, sizes),
        grid=(sizes.windows,),
        in_specs=moved + [whole(value.shape) for value in middle[2:]],
        out_specs=moved + [whole(value.shape) for value in smalls],
        out_shape=big + smalls,
        compiler_params=pltpu.CompilerParams(vmem_limit_bytes=60 * 2**20),
        name="hand_out",
    )(*middle)
    result, grad = outs[:2]
    return (result[None], grad[None]) + tuple(
        out.reshape(-1) if out.shape[0] == 1 else out for out in outs[2:]
    )


def solution(mesh):
    split = P("frame", "pix", None)
    return jax.shard_map(
        local,
        mesh=mesh,
        in_specs=(split, split, P("pix")) + (P(),) * 17,
        out_specs=(split, split) + (P(),) * 16,
        check_vma=False,
    )
```

profile of v0, /device:TPU:0, one launch (start us, length us, event | category | flops | bytes accessed | tf_op | source)
XLA Modules:
  0.0 134.0 jit_solution(13050888652419827734)
XLA Ops:
  1.3 126.8 %layer.1 = (bf16[4608,128]{1,0:T(8,128)(2,1)}, f32[4608,128]{1,0:T(8,128)}, bf16[2,16,96,128]{3,2,1,0:T(8,128)(2,1)}, bf16[2,16,16,128]{3,2,1,0:T(8,128)(2,1)}, ...) custom-call(bf16[4608,128]{1,0:T(8,128)(2,1)} %bitcast.17, bf16[4608,128]{1,0:T(8,128)(2,1)} %bitcast.18, ...), custom_call_target="tpu_custom_call" | custom-call | tf_op jit(solution)/shard_map/layer/pallas_call | solution.py:732
  128.1 5.7 %hand_out.1 = (bf16[4608,128]{1,0:T(8,128)(2,1)}, f32[4608,128]{1,0:T(8,128)}, f32[128,128]{1,0:T(8,128)}, f32[128,128]{1,0:T(8,128)}, f32[128,128]{1,0:T(8,128)...) custom-call(bf16[4608,128]{1,0:T(8,128)(2,1)} %get-tuple-element.42., ...), custom_call_target="tpu_custom_call" | custom-call | tf_op jit(solution)/shard_map/hand_out/pallas_call | solution.py:751
where the time goes:
time: 134 us
  Pallas kernels  132 us (99%)
  between operations  1.48 us (1%)
    pallas_call x1, Pallas kernels, local(): pl.pallas_call(functools.partial(layer_kernel, sizes), in_specs=[small, s...  127 us
    pallas_call x1, Pallas kernels, local(): pl.pallas_call(functools.partial(hand_out, sizes), grid=(sizes.windows,),...  5.68 us

commit v1 on v0

--- a/solution.py
+++ b/solution.py
@@ -68,7 +68,7 @@
     "x", "cot", "slot", "crop", "sq", "sk", "sv", "sm", "sgain", "sbias",
     "cq", "ck", "cv", "cm", "cgain", "cbias", "we", "ws", "fgain", "fbias",
 )
-OUTPUTS = ("result", "grad", "feed_out", "cross_out", "self_out", "totals")
+OUTPUTS = ("result", "grad", "early_out", "late_out", "totals")
 VECTORS = ("sgain", "sbias", "cgain", "cbias", "fgain", "fbias")
 
 
@@ -142,10 +142,8 @@
             send_sem=r.sem_b.at[0, w], recv_sem=r.sem_b.at[1, w], device_id=partner, device_id_type=MESH,
         )
 
-    def store_rows(target, stage, w, sem, back=None):
-        place = w if back is None else lax.rem(w, 2)
-        w = w if back is None else w + back
-        return pltpu.make_async_copy(stage.at[rows_at(place), :], target.at[rows_at(w), :], sem.at[w])
+    def store_rows(target, stage, w, sem):
+        return pltpu.make_async_copy(stage.at[rows_at(w), :], target.at[rows_at(w), :], sem.at[w])
 
     def attend(w, exps, out, inverse):
         bufs = (r.buf_a, r.buf_b)
@@ -164,7 +162,7 @@
 
         def output_part(t, rows, total):
             first, size = TILES[t]
-            part = nn(r.v_aug[:, rows], exps[w, rows, first : first + size])
+            part = nn(r.v_aug[:, rows], exps[rows, first : first + size])
             return part if total is None else total + part
 
         def output(t, both):
@@ -181,7 +179,7 @@
                 rows = slice(start, start + count)
                 if t:
                     total = output_part(t - 1, rows, total)
-                exps[w, rows, first : first + size] = jnp.exp2(
+                exps[rows, first : first + size] = jnp.exp2(
                     bufs[t % 2][rows, :size] * scale - top
                 ).astype(BF16)
             if t:
@@ -190,23 +188,23 @@
         last = len(TILES) - 1
         output(last, output_part(last, slice(0, WSLOT), None))
 
-    def attend_back(w, exps):
+    def attend_back(w, exps, dqkv):
         def query(t):
             first, size = TILES[t]
             cols = slice(first, first + size)
-            r.dqkv[:width, cols] = (nn(r.k_t[...], r.diff[:, cols]) * factor).astype(BF16)
+            dqkv[:width, cols] = (nn(r.k_t[...], r.diff[:, cols]) * factor).astype(BF16)
 
         for t, (first, size) in enumerate(TILES):
             cols = slice(first, first + size)
             grad = nn(r.v[...], r.up[:, cols]) - r.inner[:, cols]
-            r.diff[:, cols] = exps[w, :, cols] * grad.astype(BF16)
+            r.diff[:, cols] = exps[:, cols] * grad.astype(BF16)
             if t:
                 query(t - 1)
-        grad_value = nt(exps[w], r.up[...])
+        grad_value = nt(exps[...], r.up[...])
         query(len(TILES) - 1)
         grad_key = nt(r.diff[...], r.q_t[:, cols_at(w)]) * factor
-        r.dqkv[2 * width :, :] = grad_value.T.astype(BF16)
-        r.dqkv[width : 2 * width, :] = grad_key.T.astype(BF16)
+        dqkv[2 * width :, :] = grad_value.T.astype(BF16)
+        dqkv[width : 2 * width, :] = grad_key.T.astype(BF16)
 
     def forward_self(w, carry):
         x = r.x[rows_at(w), :]
@@ -214,7 +212,7 @@
         r.q_t[:, cols_at(w)] = stacked[:width]
         r.v_aug[:width, :] = stacked[width:]
         r.k[...] = nn(x, r.sk[...]).astype(BF16)
-        attend(w, r.exps, r.out_one, r.inverse_one)
+        attend(w, r.exps.at[w], r.out_one, r.inverse_one)
         merged = nn(r.self_merge_t[...], r.out_one[:, cols_at(w)])
         x_t = nt(r.eye[...], r.x[rows_at(w), :])
         for start in range(0, WSLOT, CHUNK):
@@ -243,22 +241,19 @@
     r.expand_t[...] = flip(r.we[...])
     r.shrink_t[...] = flip(r.ws[...])
 
-    def forward_cross(w, carry):
+    def forward_cross(w):
         r.q_t[:, cols_at(w)] = nn(r.cross_q_t[...], r.concat[:width, cols_at(w)]).astype(BF16)
         send_rows(w).wait()
         other = r.other[rows_at(w), :]
         r.v_aug[:width, :] = nt(r.cross_v_t[...], other).astype(BF16)
         r.k[...] = nn(other, r.ck[...]).astype(BF16)
-        attend(w, r.exps_two, r.out_two, r.inverse_two)
+        attend(w, r.exps_two.at[lax.rem(w, 2)], r.out_two, r.inverse_two)
         merged = nn(r.cross_merge_t[...], r.out_two[:, cols_at(w)])
         for start in range(0, WSLOT, CHUNK):
             hat, _ = norm_stats(merged[:, start : start + CHUNK])
             r.concat[width:, cols_at(w, start, CHUNK)] = (
                 hat * vector("cgain") + vector("cbias")
             ).astype(BF16)
-        return carry
-
-    lax.fori_loop(0, windows, forward_cross, 0)
 
     spans = sizes.rows // SPAN
 
@@ -298,51 +293,45 @@
     def add(total, part):
         return part if total is None else total + part
 
-    for name in ("act", "slope", "branch"):
-        getattr(r, name)[2] = jnp.zeros(getattr(r, name).shape[1:], BF16)
-    expand(0)
-    for rows in parts:
-        activate(0, rows)
-
-    def feed(j, carry):
-        for b in range(3):
-            i = 3 * j + b
-            old = (b + 2) % 3
-            before = jnp.maximum(i - 1, 0)
-            expand(jnp.minimum(i + 1, spans - 1))
-            hide(old)
-            branch, total = None, None
-            for rows in parts:
-                branch = add(branch, nn(r.shrink_t[:, rows], r.act[b, rows, :]))
-                total = add(total, nn(r.we[:, rows], r.hid[rows, :]))
-                activate((b + 1) % 3, rows)
-            settle(before, total)
-            up_all = nt(r.eye[...], r.cot[span(i), :])
-            for_shrink = nt(r.act[old], r.branch[old])
-            norm_tile(i, b, branch, up_all, 0)
-            for_expand = nt(r.hid[...], r.concat[:, span(before)])
-            norm_tile(i, b, branch, up_all, CHUNK)
-            r.g_ws[...] += for_shrink
-            r.g_we[...] += for_expand
-        return carry
-
-    lax.fori_loop(0, spans // 3, feed, 0)
-    last = (spans - 1) % 3
-    hide(last)
-    settle(spans - 1, nn(r.we[...], r.hid[...]))
-    r.g_ws[...] += nt(r.act[last], r.branch[last])
-    r.g_we[...] += nt(r.hid[...], r.concat[:, span(spans - 1)])
-
-    def store_result(w, carry):
-        store_rows(r.result, r.result_stage, w, r.sem_result).start()
-        return carry
-
-    lax.fori_loop(0, windows, store_result, 0)
-
-    feed_sum = Reduction(r, sizes.plans["feed"], "feed", sizes.scale, sibling, peer, core, me)
-    cross_sum = Reduction(r, sizes.plans["cross"], "cross", sizes.scale, sibling, peer, core, me)
-    self_sum = Reduction(r, sizes.plans["self"], "self", sizes.scale, sibling, peer, core, me)
-    feed_sum.begin([r.g_we.at[:, pl.ds(0, width)], r.g_we.at[:, pl.ds(width, width)], r.g_ws])
+    per_half = 2 * WSLOT // SPAN
+
+    def feed_forward(half):
+        first = per_half * half
+        for name in ("act", "slope", "branch"):
+            getattr(r, name)[2] = jnp.zeros(getattr(r, name).shape[1:], BF16)
+        expand(first)
+        for rows in parts:
+            activate(0, rows)
+
+        def feed(j, carry):
+            for b in range(3):
+                i = first + 3 * j + b
+                old = (b + 2) % 3
+                before = jnp.maximum(i - 1, first)
+                expand(jnp.minimum(i + 1, spans - 1))
+                hide(old)
+                branch, total = None, None
+                for rows in parts:
+                    branch = add(branch, nn(r.shrink_t[:, rows], r.act[b, rows, :]))
+                    total = add(total, nn(r.we[:, rows], r.hid[rows, :]))
+                    activate((b + 1) % 3, rows)
+                settle(before, total)
+                up_all = nt(r.eye[...], r.cot[span(i), :])
+                for_shrink = nt(r.act[old], r.branch[old])
+                norm_tile(i, b, branch, up_all, 0)
+                for_expand = nt(r.hid[...], r.concat[:, span(before)])
+                norm_tile(i, b, branch, up_all, CHUNK)
+                r.g_ws[...] += for_shrink
+                r.g_we[...] += for_expand
+            return carry
+
+        lax.fori_loop(0, per_half // 3, feed, 0)
+        end = first + per_half - 1
+        last = (per_half - 1) % 3
+        hide(last)
+        settle(end, nn(r.we[...], r.hid[...]))
+        r.g_ws[...] += nt(r.act[last], r.branch[last])
+        r.g_we[...] += nt(r.hid[...], r.concat[:, span(end)])
 
     def upstream(w, merged, grad_at, number, gain, out, gradient, merge, inverse):
         sums = [jnp.zeros((width, CHUNK), F32)] * 2
@@ -359,15 +348,9 @@
         r.up[...] = up
         r.inner[...] = jnp.sum(up.astype(F32) * out.astype(F32), axis=0, keepdims=True)
 
-    def backward_cross(w, carry):
-        @pl.when(w == 1)
-        def _():
-            feed_sum.scatter()
-
-        @pl.when(w == windows - 1)
-        def _():
-            feed_sum.gather()
-
+    def backward_cross(w):
+        exps = r.exps_two.at[lax.rem(w, 2)]
+        dqkv = r.dqkv.at[w]
         upstream(
             w, nn(r.cross_merge_t[...], r.out_two[:, cols_at(w)]),
             lambda start: r.grad_normed[:, cols_at(w, start, CHUNK)],
@@ -376,29 +359,48 @@
         other = r.other[rows_at(w), :]
         r.k_t[...] = nt(r.cross_k_t[...], other).astype(BF16)
         r.v[...] = nn(other, r.cv[...]).astype(BF16)
-        attend_back(w, r.exps_two)
-        r.back[w] = nn(r.cross_kv[...], r.dqkv[width:, :]).astype(BF16)
+        attend_back(w, exps, dqkv)
+        r.back[w] = nn(r.cross_kv[...], dqkv[width:, :]).astype(BF16)
         send_back(w).start()
-        r.g_cqkv[:width] += nt(r.dqkv[:width, :], r.concat[:width, cols_at(w)])
-        r.g_cqkv[width:] += nn(r.dqkv[width:, :], r.other[rows_at(w), :])
-        r.x1[:, cols_at(w)] += nn(r.cq[...], r.dqkv[:width, :])
+        r.g_cqkv[:width] += nt(dqkv[:width, :], r.concat[:width, cols_at(w)])
+        r.g_cqkv[width:] += nn(dqkv[width:, :], r.other[rows_at(w), :])
+        r.x1[:, cols_at(w)] += nn(r.cq[...], dqkv[:width, :])
+
+    def middle(half, carry):
+        def before(u, carry):
+            forward_cross(2 * half + u)
+            return carry
+
+        lax.fori_loop(0, 2, before, 0)
+        feed_forward(half)
+
+        def after(u, carry):
+            store_rows(r.result, r.result_stage, 2 * half + u, r.sem_result).start()
+            backward_cross(2 * half + u)
+            return carry
+
+        lax.fori_loop(0, 2, after, 0)
         return carry
 
-    lax.fori_loop(0, windows, backward_cross, 0)
-    cross_sum.begin([r.g_cqkv, r.g_cm])
+    lax.fori_loop(0, windows // 2, middle, 0)
+
+    early = Reduction(r, sizes.plans["early"], "early", sizes.scale, sibling, peer, core, me)
+    late = Reduction(r, sizes.plans["late"], "late", sizes.scale, sibling, peer, core, me)
+    early.begin(
+        [r.g_we.at[:, pl.ds(0, width)], r.g_we.at[:, pl.ds(width, width)], r.g_ws, r.g_cqkv, r.g_cm]
+    )
 
     def backward_self(w, carry):
         @pl.when(w == 1)
         def _():
-            feed_sum.share()
-            cross_sum.scatter()
+            early.scatter()
 
         @pl.when(w == windows - 1)
         def _():
-            feed_sum.finish()
-            feed_sum.store(r.feed_out).start()
-            cross_sum.gather()
-
+            early.gather()
+
+        exps = r.exps.at[w]
+        dqkv = r.dqkv.at[w]
         x = r.x[rows_at(w), :]
         r.q_t[:, cols_at(w)] = nt(r.self_qv_t[:width, :], x).astype(BF16)
         r.k_t[...] = nt(r.self_k_t[...], x).astype(BF16)
@@ -415,46 +417,54 @@
             w, nn(r.self_merge_t[...], r.out_one[:, cols_at(w)]), grad_at,
             0, "sgain", r.out_one, r.g_sm, r.sm, r.inverse_one,
         )
-        attend_back(w, r.exps)
-        r.g_sqkv[...] += nn(r.dqkv[...], r.x[rows_at(w), :])
-
-        @pl.when(w >= 2)
-        def _():
-            store_rows(r.grad, r.grad_stage, w, r.sem_grad, -2).wait()
-
-        total = r.x1[:, cols_at(w)] + nn(r.self_qkv[...], r.dqkv[...])
-        r.grad_stage[pl.ds(pl.multiple_of(lax.rem(w, 2) * WSLOT, WSLOT), WSLOT), :] = total.T
-        store_rows(r.grad, r.grad_stage, w, r.sem_grad, 0).start()
+        attend_back(w, exps, dqkv)
+        r.g_sqkv[...] += nn(dqkv[...], r.x[rows_at(w), :])
         return carry
 
     lax.fori_loop(0, windows, backward_self, 0)
-    self_sum.begin([r.g_sqkv, r.g_sm], r.g_vec)
-    cross_sum.share()
-    self_sum.scatter()
-    cross_sum.finish()
-    cross_sum.store(r.cross_out).start()
-    self_sum.gather()
-    if self_sum.full:
-        r.totals[...] = self_sum.vector_total()
-    self_sum.share()
-    self_sum.finish()
-    self_sum.store(r.self_out).start()
-    if not self_sum.full:
-        r.totals[...] = self_sum.total[0, 0, self_sum.shard :].astype(F32)
+
+    def finish(w):
+        place = w % 2
+        stage = r.grad_stage.at[pl.ds(place * WSLOT, WSLOT), :]
+        if w >= 2:
+            store_grad(w - 2).wait()
+        stage[...] = (r.x1[:, cols_at(w)] + nn(r.self_qkv[...], r.dqkv[w])).T
+        store_grad(w).start()
+
+    def store_grad(w):
+        place = w % 2
+        return pltpu.make_async_copy(
+            r.grad_stage.at[pl.ds(place * WSLOT, WSLOT), :], r.grad.at[pl.ds(w * WSLOT, WSLOT), :],
+            r.sem_grad.at[w],
+        )
+
+    late.begin([r.g_sqkv, r.g_sm], r.g_vec)
+    early.share()
+    finish(0)
+    late.scatter()
+    early.finish()
+    early.store(r.early_out).start()
+    finish(1)
+    late.gather()
+    if late.full:
+        r.totals[...] = late.vector_total()
+    finish(2)
+    late.share()
+    finish(3)
+    late.finish()
+    late.store(r.late_out).start()
+    if not late.full:
+        r.totals[...] = late.total[0, 0, late.shard :].astype(F32)
 
     def drain(w, carry):
         store_rows(r.result, r.result_stage, w, r.sem_result).wait()
-
-        @pl.when(w >= windows - 2)
-        def _():
-            store_rows(r.grad, r.grad_stage, w, r.sem_grad, 0).wait()
-
         return carry
 
     lax.fori_loop(0, windows, drain, 0)
-    feed_sum.store(r.feed_out).wait()
-    cross_sum.store(r.cross_out).wait()
-    self_sum.store(r.self_out).wait()
+    store_grad(2).wait()
+    store_grad(3).wait()
+    early.store(r.early_out).wait()
+    late.store(r.late_out).wait()
 
 
 class Reduction:
@@ -631,7 +641,7 @@
         "received": vmem((windows, width, WSLOT), BF16),
         "grad_normed": vmem((width, rows), F32),
         "exps": vmem((windows, WSLOT, WSLOT), BF16),
-        "exps_two": vmem((windows, WSLOT, WSLOT), BF16),
+        "exps_two": vmem((2, WSLOT, WSLOT), BF16),
         "diff": vmem((WSLOT, WSLOT), BF16),
         "act": vmem((3, hidden, SPAN), BF16),
         "slope": vmem((3, hidden, SPAN), BF16),
@@ -644,7 +654,7 @@
         "v": vmem((WSLOT, width), BF16),
         "up": vmem((width, WSLOT), BF16),
         "inner": vmem((1, WSLOT), F32),
-        "dqkv": vmem((3 * width, WSLOT), BF16),
+        "dqkv": vmem((windows, 3 * width, WSLOT), BF16),
         "result_stage": vmem((rows, width), BF16),
         "grad_stage": vmem((2 * WSLOT, width), F32),
         "sem_x": dma((2, windows)),
@@ -682,9 +692,9 @@
 
 
 def hand_out(sizes, *refs):
-    result_in, grad_in, feed, cross, own, totals, result, grad = refs[:8]
+    result_in, grad_in, early, late, totals, result, grad = refs[:7]
     (o_sq, o_sk, o_sv, o_sm, o_sgain, o_sbias, o_cq, o_ck, o_cv, o_cm, o_cgain, o_cbias,
-     o_we, o_ws, o_fgain, o_fbias) = refs[8:24]
+     o_we, o_ws, o_fgain, o_fbias) = refs[7:23]
     width, hidden = sizes.width, sizes.hidden
     shards = [plan.shard for plan in sizes.plans.values()]
     result[...] = result_in[...]
@@ -692,14 +702,14 @@
 
     @pl.when(pl.program_id(0) == 0)
     def _():
-        o_we[:width, :] = total_rows(feed, shards[0], 0, hidden).astype(F32).T
-        o_we[width:, :] = total_rows(feed, shards[0], hidden, hidden).astype(F32).T
-        o_ws[...] = total_rows(feed, shards[0], 2 * hidden, hidden).astype(F32)
-        for source, shard, group in (
-            (cross, shards[1], (o_cq, o_ck, o_cv, o_cm)), (own, shards[2], (o_sq, o_sk, o_sv, o_sm))
+        o_we[:width, :] = total_rows(early, shards[0], 0, hidden).astype(F32).T
+        o_we[width:, :] = total_rows(early, shards[0], hidden, hidden).astype(F32).T
+        o_ws[...] = total_rows(early, shards[0], 2 * hidden, hidden).astype(F32)
+        for source, shard, base, group in (
+            (early, shards[0], 3 * hidden, (o_cq, o_ck, o_cv, o_cm)), (late, shards[1], 0, (o_sq, o_sk, o_sv, o_sm))
         ):
             for i, ref in enumerate(group):
-                total = total_rows(source, shard, i * width, width).astype(F32)
+                total = total_rows(source, shard, base + i * width, width).astype(F32)
                 ref[...] = total if i == 3 else total.T
         for i, ref in enumerate((o_sgain, o_sbias, o_cgain, o_cbias, o_fgain, o_fbias)):
             ref[...] = totals[i : i + 1, :]
@@ -719,7 +729,7 @@
     sizes = types.SimpleNamespace(
         rows=rows, width=width, hidden=hidden, windows=rows // WSLOT, peers=peers,
         scale=1.0 / math.sqrt(2.0 * rows * peers),
-        plans={"feed": plan(3 * hidden), "cross": plan(4 * width), "self": plan(4 * width, 16)},
+        plans={"early": plan(3 * hidden + 4 * width), "late": plan(4 * width, 16)},
     )
     flat = lambda value: value.reshape(1, -1) if value.ndim == 1 else value
     shape = jax.ShapeDtypeStruct
@@ -732,7 +742,7 @@
     middle = pl.pallas_call(
         functools.partial(layer_kernel, sizes),
         in_specs=[small, small, scalar, scalar] + [small] * 16,
-        out_specs=[large] * 5 + [small],
+        out_specs=[large] * 4 + [small],
         out_shape=big + [
             shape((2, plan.owners, plan.kept, width), BF16) for plan in sizes.plans.values()
         ] + [shape((16, width), F32)],

time: 134 us -> 123 us (0.918)
  Pallas kernels: 132 us -> 121 us
    pallas_call x1, Pallas kernels: 127 us -> 116 us  [local(): pl.pallas_call(functools.partial(layer_kernel, sizes), in_specs=[small, s...]
where the time goes in v1:
time: 123 us
  Pallas kernels  121 us (98%)
  between operations  1.5 us (1%)
    pallas_call x1, Pallas kernels, local(): pl.pallas_call(functools.partial(layer_kernel, sizes), in_specs=[small, s...  116 us
    pallas_call x1, Pallas kernels, local(): pl.pallas_call(functools.partial(hand_out, sizes), grid=(sizes.windows,),...  5.71 us

profile of v1, /device:TPU:0, one launch (start us, length us, event | category | flops | bytes accessed | tf_op | source)
XLA Modules:
  0.0 122.9 jit_solution(11436421560120490389)
XLA Ops:
  1.3 115.7 %layer.1 = (bf16[4608,128]{1,0:T(8,128)(2,1)}, f32[4608,128]{1,0:T(8,128)}, bf16[2,16,112,128]{3,2,1,0:T(8,128)(2,1)}, bf16[2,16,16,128]{3,2,1,0:T(8,128)(2,1)}, f32[16,128]{1,0:T(8,128)}) custom-call(bf16[4608,128]{1,0:T(8,128)(2,1)} %bitcast.17, bf16[4608,128]{1,0:T(8,128)(2,1)} %bitcast.18, s32[1]{0:T(128)S(6)} %copy.38.refs_2_, s32[2,16]{1,0:T(2,128)} %bitcast.19, ...), custom_call_target="tpu_custom_call" | custom-call | tf_op jit(solution)/shard_map/layer/pallas_call | solution.py:742
  117.1 5.7 %hand_out.1 = (bf16[4608,128]{1,0:T(8,128)(2,1)}, f32[4608,128]{1,0:T(8,128)}, f32[128,128]{1,0:T(8,128)}, f32[128,128]{1,0:T(8,128)}, f32[128,128]{1,0:T(8,128)...) custom-call(bf16[4608,128]{1,0:T(8,128)(2,1)} %get-tuple-element.41., ...), custom_call_target="tpu_custom_call" | custom-call | tf_op jit(solution)/shard_map/hand_out/pallas_call | solution.py:761

commit v2 on v1

--- a/solution.py
+++ b/solution.py
@@ -58,6 +58,14 @@
     tail = poly * t * bell
     phi = jnp.where(low >= BF16(0.0), BF16(1.0) - tail, tail)
     return low * phi, phi + low * bell * BF16(1.0 / math.sqrt(2.0 * math.pi))
+
+
+def weave(main, *others):
+    order = [((i + 0.5) / len(main), step) for i, step in enumerate(main)]
+    for first, last, steps in others:
+        order += [(first + (last - first) * (i + 0.5) / len(steps), step) for i, step in enumerate(steps)]
+    for _, step in sorted(order, key=lambda entry: entry[0]):
+        step()
 
 
 def flip(values):
@@ -118,7 +126,7 @@
     vector = lambda name: r.vectors[VECTORS.index(name)]
     for name in ("g_sqkv", "g_sm", "g_cqkv", "g_cm", "g_we", "g_ws", "g_vec"):
         getattr(r, name)[...] = jnp.zeros_like(getattr(r, name))
-    r.v_aug[width:, :] = jnp.ones((ONES, WSLOT), BF16)
+    r.v_aug[:, width:, :] = jnp.ones((2, ONES, WSLOT), BF16)
 
     def alive_at(start, size):
         token = lax.broadcasted_iota(jnp.int32, (1, size), 1) + lax.rem(start, WSLOT)
@@ -145,92 +153,135 @@
     def store_rows(target, stage, w, sem):
         return pltpu.make_async_copy(stage.at[rows_at(w), :], target.at[rows_at(w), :], sem.at[w])
 
-    def attend(w, exps, out, inverse):
+    def attend(w, u, exps, out, inverse):
         bufs = (r.buf_a, r.buf_b)
+        tops, sums = {}, {}
 
         def score(t):
             first, size = TILES[t]
-            got = nn(r.k[...], r.q_t[:, cols_at(w, first, size)])
+            got = nn(r.k[u], r.q_t[:, cols_at(w, first, size)])
             rest = got[FEWEST:]
             row = lax.broadcasted_iota(jnp.int32, rest.shape, 0) + FEWEST
             rest = jnp.where(row < live, rest, NEGATIVE)
             bufs[t % 2][:FEWEST, :size] = got[:FEWEST]
             bufs[t % 2][FEWEST:, :size] = rest
-            return scale * jnp.maximum(
+            tops[t] = scale * jnp.maximum(
                 jnp.max(got[:FEWEST], axis=0, keepdims=True), jnp.max(rest, axis=0, keepdims=True)
             )
 
-        def output_part(t, rows, total):
+        def output_part(t, rows):
             first, size = TILES[t]
-            part = nn(r.v_aug[:, rows], exps[rows, first : first + size])
-            return part if total is None else total + part
-
-        def output(t, both):
+            part = nn(r.v_aug[u, :, rows], exps[rows, first : first + size])
+            sums[t] = part if t not in sums else sums[t] + part
+
+        def output(t):
             first, size = TILES[t]
+            both = sums[t]
             share = 1.0 / both[width : width + 1]
             inverse[:, cols_at(w, first, size)] = share
             out[:, cols_at(w, first, size)] = (both[:width] * share).astype(BF16)
 
-        top = score(0)
-        for t, (first, size) in enumerate(TILES):
-            after = score(t + 1) if t + 1 < len(TILES) else None
-            total = None
-            for start, count in TILES:
-                rows = slice(start, start + count)
-                if t:
-                    total = output_part(t - 1, rows, total)
-                exps[rows, first : first + size] = jnp.exp2(
-                    bufs[t % 2][rows, :size] * scale - top
-                ).astype(BF16)
+        def soften(t, start, count):
+            first, size = TILES[t]
+            rows = slice(start, start + count)
             if t:
-                output(t - 1, total)
-            top = after
+                output_part(t - 1, rows)
+            exps[rows, first : first + size] = jnp.exp2(
+                bufs[t % 2][rows, :size] * scale - tops[t]
+            ).astype(BF16)
+
         last = len(TILES) - 1
-        output(last, output_part(last, slice(0, WSLOT), None))
-
-    def attend_back(w, exps, dqkv):
+        steps = [functools.partial(score, 0)]
+        for t in range(len(TILES)):
+            if t < last:
+                steps.append(functools.partial(score, t + 1))
+            steps += [functools.partial(soften, t, start, count) for start, count in TILES]
+            if t:
+                steps.append(functools.partial(output, t - 1))
+        return steps + [
+            functools.partial(output_part, last, slice(0, WSLOT)), functools.partial(output, last)
+        ]
+
+    def attend_back(w, u, exps, dqkv):
+        kept = {}
+
+        def differ(t):
+            first, size = TILES[t]
+            cols = slice(first, first + size)
+            grad = nn(r.v[u], r.up[u, :, cols]) - r.inner[u, :, cols]
+            r.diff[:, cols] = exps[:, cols] * grad.astype(BF16)
+
         def query(t):
             first, size = TILES[t]
             cols = slice(first, first + size)
-            dqkv[:width, cols] = (nn(r.k_t[...], r.diff[:, cols]) * factor).astype(BF16)
-
-        for t, (first, size) in enumerate(TILES):
-            cols = slice(first, first + size)
-            grad = nn(r.v[...], r.up[:, cols]) - r.inner[:, cols]
-            r.diff[:, cols] = exps[:, cols] * grad.astype(BF16)
-            if t:
-                query(t - 1)
-        grad_value = nt(exps[...], r.up[...])
-        query(len(TILES) - 1)
-        grad_key = nt(r.diff[...], r.q_t[:, cols_at(w)]) * factor
-        dqkv[2 * width :, :] = grad_value.T.astype(BF16)
-        dqkv[width : 2 * width, :] = grad_key.T.astype(BF16)
-
-    def forward_self(w, carry):
-        x = r.x[rows_at(w), :]
-        stacked = nt(r.self_qv_t[...], x).astype(BF16)
-        r.q_t[:, cols_at(w)] = stacked[:width]
-        r.v_aug[:width, :] = stacked[width:]
-        r.k[...] = nn(x, r.sk[...]).astype(BF16)
-        attend(w, r.exps.at[w], r.out_one, r.inverse_one)
-        merged = nn(r.self_merge_t[...], r.out_one[:, cols_at(w)])
-        x_t = nt(r.eye[...], r.x[rows_at(w), :])
-        for start in range(0, WSLOT, CHUNK):
+            dqkv[:width, cols] = (nn(r.k_t[u], r.diff[:, cols]) * factor).astype(BF16)
+
+        def value():
+            kept["v"] = nt(exps[...], r.up[u])
+
+        def key():
+            kept["k"] = nt(r.diff[...], r.q_t[:, cols_at(w)]) * factor
+
+        def turn_value():
+            dqkv[2 * width :, :] = kept["v"].T.astype(BF16)
+
+        def turn_key():
+            dqkv[width : 2 * width, :] = kept["k"].T.astype(BF16)
+
+        steps = [functools.partial(differ, 0)]
+        for t in range(1, len(TILES)):
+            steps += [functools.partial(differ, t), functools.partial(query, t - 1)]
+        return steps + [
+            value, functools.partial(query, len(TILES) - 1), key, turn_value, turn_key
+        ]
+
+    def prepare_self(w, u):
+        def project():
+            stacked = nt(r.self_qv_t[...], r.x[rows_at(w), :]).astype(BF16)
+            r.q_t[:, cols_at(w)] = stacked[:width]
+            r.v_aug[u, :width, :] = stacked[width:]
+
+        def keys():
+            r.k[u] = nn(r.x[rows_at(w), :], r.sk[...]).astype(BF16)
+
+        return [project, keys]
+
+    def conclude_self(w):
+        kept = {}
+
+        def merge():
+            kept["m"] = nn(r.self_merge_t[...], r.out_one[:, cols_at(w)])
+            kept["x"] = nt(r.eye[...], r.x[rows_at(w), :])
+
+        def norm(start):
             cols = slice(start, start + CHUNK)
-            hat, _ = norm_stats(merged[:, cols])
-            x1 = x_t[:, cols] + hat * vector("sgain") + vector("sbias")
+            hat, _ = norm_stats(kept["m"][:, cols])
+            x1 = kept["x"][:, cols] + hat * vector("sgain") + vector("sbias")
             r.x1[:, cols_at(w, start, CHUNK)] = x1
             r.concat[:width, cols_at(w, start, CHUNK)] = x1.astype(BF16)
             r.send[pl.ds(pl.multiple_of(w * WSLOT + start, CHUNK), CHUNK), :] = x1.T.astype(BF16)
 
-        @pl.when(w == 0)
+        chunks = [functools.partial(norm, start) for start in range(0, WSLOT, CHUNK)]
+        return [merge] + chunks + [send_rows(w).start]
+
+    def forward_self(p, carry):
+        w = 2 * p
+        weave(prepare_self(w, 0))
+        weave(
+            attend(w, 0, r.exps.at[w], r.out_one, r.inverse_one), (0.5, 1.0, prepare_self(w + 1, 1))
+        )
+
+        @pl.when(p == 0)
         def _():
             pl.semaphore_wait(barrier, peers)
 
-        send_rows(w).start()
+        weave(
+            attend(w + 1, 1, r.exps.at[w + 1], r.out_one, r.inverse_one), (0.0, 0.8, conclude_self(w))
+        )
+        weave(conclude_self(w + 1))
         return carry
 
-    lax.fori_loop(0, windows, forward_self, 0)
+    lax.fori_loop(0, windows // 2, forward_self, 0)
 
     r.cross_q_t[...] = flip(r.cq[...])
     r.cross_k_t[...] = flip(r.ck[...])
@@ -241,19 +292,42 @@
     r.expand_t[...] = flip(r.we[...])
     r.shrink_t[...] = flip(r.ws[...])
 
-    def forward_cross(w):
-        r.q_t[:, cols_at(w)] = nn(r.cross_q_t[...], r.concat[:width, cols_at(w)]).astype(BF16)
-        send_rows(w).wait()
-        other = r.other[rows_at(w), :]
-        r.v_aug[:width, :] = nt(r.cross_v_t[...], other).astype(BF16)
-        r.k[...] = nn(other, r.ck[...]).astype(BF16)
-        attend(w, r.exps_two.at[lax.rem(w, 2)], r.out_two, r.inverse_two)
-        merged = nn(r.cross_merge_t[...], r.out_two[:, cols_at(w)])
-        for start in range(0, WSLOT, CHUNK):
-            hat, _ = norm_stats(merged[:, start : start + CHUNK])
+    def prepare_cross(w, u):
+        def queries():
+            r.q_t[:, cols_at(w)] = nn(r.cross_q_t[...], r.concat[:width, cols_at(w)]).astype(BF16)
+
+        def values():
+            send_rows(w).wait()
+            r.v_aug[u, :width, :] = nt(r.cross_v_t[...], r.other[rows_at(w), :]).astype(BF16)
+
+        def keys():
+            r.k[u] = nn(r.other[rows_at(w), :], r.ck[...]).astype(BF16)
+
+        return [queries, values, keys]
+
+    def conclude_cross(w):
+        kept = {}
+
+        def merge():
+            kept["m"] = nn(r.cross_merge_t[...], r.out_two[:, cols_at(w)])
+
+        def norm(start):
+            hat, _ = norm_stats(kept["m"][:, start : start + CHUNK])
             r.concat[width:, cols_at(w, start, CHUNK)] = (
                 hat * vector("cgain") + vector("cbias")
             ).astype(BF16)
+
+        return [merge] + [functools.partial(norm, start) for start in range(0, WSLOT, CHUNK)]
+
+    def forward_cross(w):
+        weave(prepare_cross(w, 0))
+        weave(
+            attend(w, 0, r.exps_two.at[0], r.out_two, r.inverse_two), (0.6, 1.0, prepare_cross(w + 1, 1))
+        )
+        weave(
+            attend(w + 1, 1, r.exps_two.at[1], r.out_two, r.inverse_two), (0.0, 0.8, conclude_cross(w))
+        )
+        weave(conclude_cross(w + 1))
 
     spans = sizes.rows // SPAN
 
@@ -333,53 +407,82 @@
         r.g_ws[...] += nt(r.act[last], r.branch[last])
         r.g_we[...] += nt(r.hid[...], r.concat[:, span(end)])
 
-    def upstream(w, merged, grad_at, number, gain, out, gradient, merge, inverse):
-        sums = [jnp.zeros((width, CHUNK), F32)] * 2
-        for start in range(0, WSLOT, CHUNK):
-            hat, root = norm_stats(merged[:, start : start + CHUNK])
+    def upstream(w, u, merge_t, grad_at, number, gain, out, gradient, merge, inverse):
+        kept = {"sums": [jnp.zeros((width, CHUNK), F32)] * 2}
+
+        def remake():
+            kept["m"] = nn(merge_t[...], out[:, cols_at(w)])
+
+        def back(start):
+            hat, root = norm_stats(kept["m"][:, start : start + CHUNK])
             grad = grad_at(start)
-            sums = [sums[0] + grad * hat, sums[1] + grad]
-            r.grad_merged[:, start : start + CHUNK] = norm_back(hat, root, vector(gain), grad).astype(BF16)
-        r.g_vec[number] += sums[0]
-        r.g_vec[number + 1] += sums[1]
-        out = out[:, cols_at(w)]
-        gradient[...] += nt(out, r.grad_merged[...])
-        up = (nn(merge[...], r.grad_merged[...]) * inverse[:, cols_at(w)]).astype(BF16)
-        r.up[...] = up
-        r.inner[...] = jnp.sum(up.astype(F32) * out.astype(F32), axis=0, keepdims=True)
+            sums = kept["sums"]
+            kept["sums"] = [sums[0] + grad * hat, sums[1] + grad]
+            r.grad_merged[u, :, start : start + CHUNK] = norm_back(
+                hat, root, vector(gain), grad
+            ).astype(BF16)
+
+        def add_up():
+            r.g_vec[number] += kept["sums"][0]
+            r.g_vec[number + 1] += kept["sums"][1]
+            kept["up"] = nn(merge[...], r.grad_merged[u])
+
+        def collect():
+            gradient[...] += nt(out[:, cols_at(w)], r.grad_merged[u])
+
+        def lift():
+            up = (kept["up"] * inverse[:, cols_at(w)]).astype(BF16)
+            r.up[u] = up
+            r.inner[u] = jnp.sum(
+                up.astype(F32) * out[:, cols_at(w)].astype(F32), axis=0, keepdims=True
+            )
+
+        chunks = [functools.partial(back, start) for start in range(0, WSLOT, CHUNK)]
+        return [remake] + chunks + [add_up, collect, lift]
+
+    def unfold_cross(w, u):
+        def keys():
+            r.k_t[u] = nt(r.cross_k_t[...], r.other[rows_at(w), :]).astype(BF16)
+
+        def values():
+            r.v[u] = nn(r.other[rows_at(w), :], r.cv[...]).astype(BF16)
+
+        steps = upstream(
+            w, u, r.cross_merge_t, lambda start: r.grad_normed[:, cols_at(w, start, CHUNK)],
+            2, "cgain", r.out_two, r.g_cm, r.cm, r.inverse_two,
+        )
+        return [steps[0], keys, values] + steps[1:]
+
+    def deliver_cross(w):
+        def back():
+            r.back[w] = nn(r.cross_kv[...], r.dqkv[w, width:, :]).astype(BF16)
+            send_back(w).start()
+
+        def queries():
+            r.g_cqkv[:width] += nt(r.dqkv[w, :width, :], r.concat[:width, cols_at(w)])
+
+        def others():
+            r.g_cqkv[width:] += nn(r.dqkv[w, width:, :], r.other[rows_at(w), :])
+
+        def inputs():
+            r.x1[:, cols_at(w)] += nn(r.cq[...], r.dqkv[w, :width, :])
+
+        return [back, queries, others, inputs]
 
     def backward_cross(w):
-        exps = r.exps_two.at[lax.rem(w, 2)]
-        dqkv = r.dqkv.at[w]
-        upstream(
-            w, nn(r.cross_merge_t[...], r.out_two[:, cols_at(w)]),
-            lambda start: r.grad_normed[:, cols_at(w, start, CHUNK)],
-            2, "cgain", r.out_two, r.g_cm, r.cm, r.inverse_two,
-        )
-        other = r.other[rows_at(w), :]
-        r.k_t[...] = nt(r.cross_k_t[...], other).astype(BF16)
-        r.v[...] = nn(other, r.cv[...]).astype(BF16)
-        attend_back(w, exps, dqkv)
-        r.back[w] = nn(r.cross_kv[...], dqkv[width:, :]).astype(BF16)
-        send_back(w).start()
-        r.g_cqkv[:width] += nt(dqkv[:width, :], r.concat[:width, cols_at(w)])
-        r.g_cqkv[width:] += nn(dqkv[width:, :], r.other[rows_at(w), :])
-        r.x1[:, cols_at(w)] += nn(r.cq[...], dqkv[:width, :])
+        weave(unfold_cross(w, 0))
+        weave(
+            attend_back(w, 0, r.exps_two.at[0], r.dqkv.at[w]), (0.0, 0.9, unfold_cross(w + 1, 1))
+        )
+        weave(attend_back(w + 1, 1, r.exps_two.at[1], r.dqkv.at[w + 1]), (0.0, 0.5, deliver_cross(w)))
+        weave(deliver_cross(w + 1))
 
     def middle(half, carry):
-        def before(u, carry):
-            forward_cross(2 * half + u)
-            return carry
-
-        lax.fori_loop(0, 2, before, 0)
+        forward_cross(2 * half)
         feed_forward(half)
-
-        def after(u, carry):
+        for u in range(2):
             store_rows(r.result, r.result_stage, 2 * half + u, r.sem_result).start()
-            backward_cross(2 * half + u)
-            return carry
-
-        lax.fori_loop(0, 2, after, 0)
+        backward_cross(2 * half)
         return carry
 
     lax.fori_loop(0, windows // 2, middle, 0)
@@ -390,22 +493,16 @@
         [r.g_we.at[:, pl.ds(0, width)], r.g_we.at[:, pl.ds(width, width)], r.g_ws, r.g_cqkv, r.g_cm]
     )
 
-    def backward_self(w, carry):
-        @pl.when(w == 1)
-        def _():
-            early.scatter()
-
-        @pl.when(w == windows - 1)
-        def _():
-            early.gather()
-
-        exps = r.exps.at[w]
-        dqkv = r.dqkv.at[w]
-        x = r.x[rows_at(w), :]
-        r.q_t[:, cols_at(w)] = nt(r.self_qv_t[:width, :], x).astype(BF16)
-        r.k_t[...] = nt(r.self_k_t[...], x).astype(BF16)
-        r.v[...] = nn(x, r.sv[...]).astype(BF16)
-        send_back(w).wait()
+    def unfold_self(w, u):
+        def queries():
+            r.q_t[:, cols_at(w)] = nt(r.self_qv_t[:width, :], r.x[rows_at(w), :]).astype(BF16)
+
+        def keys():
+            r.k_t[u] = nt(r.self_k_t[...], r.x[rows_at(w), :]).astype(BF16)
+
+        def values():
+            r.v[u] = nn(r.x[rows_at(w), :], r.sv[...]).astype(BF16)
+            send_back(w).wait()
 
         def grad_at(start):
             here = cols_at(w, start, CHUNK)
@@ -413,15 +510,37 @@
             r.x1[:, here] = grad
             return grad
 
-        upstream(
-            w, nn(r.self_merge_t[...], r.out_one[:, cols_at(w)]), grad_at,
-            0, "sgain", r.out_one, r.g_sm, r.sm, r.inverse_one,
-        )
-        attend_back(w, exps, dqkv)
-        r.g_sqkv[...] += nn(dqkv[...], r.x[rows_at(w), :])
+        steps = upstream(
+            w, u, r.self_merge_t, grad_at, 0, "sgain", r.out_one, r.g_sm, r.sm, r.inverse_one
+        )
+        return [steps[0], queries, keys, values] + steps[1:]
+
+    def deliver_self(w):
+        def all_three():
+            r.g_sqkv[...] += nn(r.dqkv[w], r.x[rows_at(w), :])
+
+        return [all_three]
+
+    def backward_self(p, carry):
+        w = 2 * p
+        weave(unfold_self(w, 0))
+        weave(attend_back(w, 0, r.exps.at[w], r.dqkv.at[w]), (0.0, 0.9, unfold_self(w + 1, 1)))
+
+        @pl.when(p == 0)
+        def _():
+            early.scatter()
+
+        @pl.when(p == 1)
+        def _():
+            early.gather()
+
+        weave(
+            attend_back(w + 1, 1, r.exps.at[w + 1], r.dqkv.at[w + 1]), (0.0, 0.5, deliver_self(w))
+        )
+        weave(deliver_self(w + 1))
         return carry
 
-    lax.fori_loop(0, windows, backward_self, 0)
+    lax.fori_loop(0, windows // 2, backward_self, 0)
 
     def finish(w):
         place = w % 2
@@ -627,8 +746,8 @@
         "g_ws": vmem((hidden, width), F32),
         "g_vec": vmem((len(VECTORS), width, CHUNK), F32),
         "q_t": vmem((width, rows), BF16),
-        "k": vmem((WSLOT, width), BF16),
-        "v_aug": vmem((width + ONES, WSLOT), BF16),
+        "k": vmem((2, WSLOT, width), BF16),
+        "v_aug": vmem((2, width + ONES, WSLOT), BF16),
         "out_one": vmem((width, rows), BF16),
         "out_two": vmem((width, rows), BF16),
         "inverse_one": vmem((1, rows), F32),
@@ -649,11 +768,11 @@
         "hid": vmem((hidden, SPAN), BF16),
         "buf_a": vmem((max(WSLOT, hidden), SPAN), F32),
         "buf_b": vmem((WSLOT, SPAN), F32),
-        "grad_merged": vmem((width, WSLOT), BF16),
-        "k_t": vmem((width, WSLOT), BF16),
-        "v": vmem((WSLOT, width), BF16),
-        "up": vmem((width, WSLOT), BF16),
-        "inner": vmem((1, WSLOT), F32),
+        "grad_merged": vmem((2, width, WSLOT), BF16),
+        "k_t": vmem((2, width, WSLOT), BF16),
+        "v": vmem((2, WSLOT, width), BF16),
+        "up": vmem((2, width, WSLOT), BF16),
+        "inner": vmem((2, 1, WSLOT), F32),
         "dqkv": vmem((windows, 3 * width, WSLOT), BF16),
         "result_stage": vmem((rows, width), BF16),
         "grad_stage": vmem((2 * WSLOT, width), F32),
@@ -700,11 +819,19 @@
     result[...] = result_in[...]
     grad[...] = grad_in[...]
 
-    @pl.when(pl.program_id(0) == 0)
+    step = pl.program_id(0)
+    quarter = hidden // sizes.windows
+    for w in range(sizes.windows):
+
+        @pl.when(step == w)
+        def _():
+            at = w * quarter
+            o_we[:width, :] = total_rows(early, shards[0], at, quarter).astype(F32).T
+            o_we[width:, :] = total_rows(early, shards[0], hidden + at, quarter).astype(F32).T
+            o_ws[...] = total_rows(early, shards[0], 2 * hidden + at, quarter).astype(F32)
+
+    @pl.when(step == 0)
     def _():
-        o_we[:width, :] = total_rows(early, shards[0], 0, hidden).astype(F32).T
-        o_we[width:, :] = total_rows(early, shards[0], hidden, hidden).astype(F32).T
-        o_ws[...] = total_rows(early, shards[0], 2 * hidden, hidden).astype(F32)
         for source, shard, base, group in (
             (early, shards[0], 3 * hidden, (o_cq, o_ck, o_cv, o_cm)), (late, shards[1], 0, (o_sq, o_sk, o_sv, o_sm))
         ):
@@ -762,7 +889,11 @@
         functools.partial(hand_out, sizes),
         grid=(sizes.windows,),
         in_specs=moved + [whole(value.shape) for value in middle[2:]],
-        out_specs=moved + [whole(value.shape) for value in smalls],
+        out_specs=moved + [whole(value.shape) for value in smalls[:12]] + [
+            pl.BlockSpec((2 * width, hidden // sizes.windows), lambda w: (0, w)),
+            pl.BlockSpec((hidden // sizes.windows, width), lambda w: (w, 0)),
+            whole(row.shape), whole(row.shape),
+        ],
         out_shape=big + smalls,
         compiler_params=pltpu.CompilerParams(vmem_limit_bytes=60 * 2**20),
         name="hand_out",

time: 123 us -> 123 us (level)
  no operation moved by 1% of the time
where the time goes in v2:
time: 123 us
  Pallas kernels  122 us (99%)
  between operations  1.49 us (1%)
    pallas_call x1, Pallas kernels, local(): pl.pallas_call(functools.partial(layer_kernel, sizes), in_specs=[small, s...  116 us
    pallas_call x1, Pallas kernels, local(): pl.pallas_call(functools.partial(hand_out, sizes), grid=(sizes.windows,),...  5.67 us

profile of v2, /device:TPU:0, one launch (start us, length us, event | category | flops | bytes accessed | tf_op | source)
XLA Modules:
  0.0 123.1 jit_solution(3127062038242596860)
XLA Ops:
  1.3 116.0 %layer.1 = (bf16[4608,128]{1,0:T(8,128)(2,1)}, f32[4608,128]{1,0:T(8,128)}, bf16[2,16,112,128]{3,2,1,0:T(8,128)(2,1)}, bf16[2,16,16,128]{3,2,1,0:T(8,128)(2,1)}, f32[16,128]{1,0:T(8,128)}) custom-call(bf16[4608,128]{1,0:T(8,128)(2,1)} %bitcast.17, bf16[4608,128]{1,0:T(8,128)(2,1)} %bitcast.18, s32[1]{0:T(128)S(6)} %copy.38.refs_2_, s32[2,16]{1,0:T(2,128)} %bitcast.19, ...), custom_call_target="tpu_custom_call" | custom-call | tf_op jit(solution)/shard_map/layer/pallas_call | solution.py:869
  117.3 5.7 %hand_out.1 = (bf16[4608,128]{1,0:T(8,128)(2,1)}, f32[4608,128]{1,0:T(8,128)}, f32[128,128]{1,0:T(8,128)}, f32[128,128]{1,0:T(8,128)}, f32[128,128]{1,0:T(8,128)...) custom-call(bf16[4608,128]{1,0:T(8,128)(2,1)} %get-tuple-element.41., ...), custom_call_target="tpu_custom_call" | custom-call | tf_op jit(solution)/shard_map/hand_out/pallas_call | solution.py:888

commit v3 on v2

--- a/solution.py
+++ b/solution.py
@@ -76,7 +76,7 @@
     "x", "cot", "slot", "crop", "sq", "sk", "sv", "sm", "sgain", "sbias",
     "cq", "ck", "cv", "cm", "cgain", "cbias", "we", "ws", "fgain", "fbias",
 )
-OUTPUTS = ("result", "grad", "early_out", "late_out", "totals")
+OUTPUTS = ("result", "grad", "feed_out", "cross_out", "late_out", "totals")
 VECTORS = ("sgain", "sbias", "cgain", "cbias", "fgain", "fbias")
 
 
@@ -474,24 +474,34 @@
         weave(
             attend_back(w, 0, r.exps_two.at[0], r.dqkv.at[w]), (0.0, 0.9, unfold_cross(w + 1, 1))
         )
+
+        @pl.when(w == windows - 2)
+        def _():
+            feed_sum.scatter()
+
         weave(attend_back(w + 1, 1, r.exps_two.at[1], r.dqkv.at[w + 1]), (0.0, 0.5, deliver_cross(w)))
         weave(deliver_cross(w + 1))
+
+    feed_sum = Reduction(r, sizes.plans["feed"], "feed", sizes.scale, sibling, peer, core, me)
+    cross_sum = Reduction(r, sizes.plans["cross"], "cross", sizes.scale, sibling, peer, core, me)
+    late = Reduction(r, sizes.plans["late"], "late", sizes.scale, sibling, peer, core, me)
 
     def middle(half, carry):
         forward_cross(2 * half)
         feed_forward(half)
         for u in range(2):
             store_rows(r.result, r.result_stage, 2 * half + u, r.sem_result).start()
+
+        @pl.when(half == windows // 2 - 1)
+        def _():
+            feed_sum.begin([r.g_we.at[:, pl.ds(0, width)], r.g_we.at[:, pl.ds(width, width)], r.g_ws])
+
         backward_cross(2 * half)
         return carry
 
     lax.fori_loop(0, windows // 2, middle, 0)
 
-    early = Reduction(r, sizes.plans["early"], "early", sizes.scale, sibling, peer, core, me)
-    late = Reduction(r, sizes.plans["late"], "late", sizes.scale, sibling, peer, core, me)
-    early.begin(
-        [r.g_we.at[:, pl.ds(0, width)], r.g_we.at[:, pl.ds(width, width)], r.g_ws, r.g_cqkv, r.g_cm]
-    )
+    cross_sum.begin([r.g_cqkv, r.g_cm])
 
     def unfold_self(w, u):
         def queries():
@@ -528,11 +538,13 @@
 
         @pl.when(p == 0)
         def _():
-            early.scatter()
+            feed_sum.gather()
+            cross_sum.scatter()
 
         @pl.when(p == 1)
         def _():
-            early.gather()
+            cross_sum.gather()
+            feed_sum.share()
 
         weave(
             attend_back(w + 1, 1, r.exps.at[w + 1], r.dqkv.at[w + 1]), (0.0, 0.5, deliver_self(w))
@@ -558,16 +570,18 @@
         )
 
     late.begin([r.g_sqkv, r.g_sm], r.g_vec)
-    early.share()
     finish(0)
     late.scatter()
-    early.finish()
-    early.store(r.early_out).start()
+    cross_sum.share()
     finish(1)
+    feed_sum.finish()
+    feed_sum.store(r.feed_out).start()
     late.gather()
     if late.full:
         r.totals[...] = late.vector_total()
     finish(2)
+    cross_sum.finish()
+    cross_sum.store(r.cross_out).start()
     late.share()
     finish(3)
     late.finish()
@@ -582,7 +596,8 @@
     lax.fori_loop(0, windows, drain, 0)
     store_grad(2).wait()
     store_grad(3).wait()
-    early.store(r.early_out).wait()
+    feed_sum.store(r.feed_out).wait()
+    cross_sum.store(r.cross_out).wait()
     late.store(r.late_out).wait()
 
 
@@ -811,29 +826,31 @@
 
 
 def hand_out(sizes, *refs):
-    result_in, grad_in, early, late, totals, result, grad = refs[:7]
+    result_in, grad_in, feed, cross, late, totals, result, grad = refs[:8]
     (o_sq, o_sk, o_sv, o_sm, o_sgain, o_sbias, o_cq, o_ck, o_cv, o_cm, o_cgain, o_cbias,
-     o_we, o_ws, o_fgain, o_fbias) = refs[7:23]
+     o_we, o_ws, o_fgain, o_fbias) = refs[8:24]
+    result_stage, grad_stage, sems = refs[24:]
     width, hidden = sizes.width, sizes.hidden
     shards = [plan.shard for plan in sizes.plans.values()]
-    result[...] = result_in[...]
-    grad[...] = grad_in[...]
-
-    step = pl.program_id(0)
-    quarter = hidden // sizes.windows
-    for w in range(sizes.windows):
-
-        @pl.when(step == w)
-        def _():
-            at = w * quarter
-            o_we[:width, :] = total_rows(early, shards[0], at, quarter).astype(F32).T
-            o_we[width:, :] = total_rows(early, shards[0], hidden + at, quarter).astype(F32).T
-            o_ws[...] = total_rows(early, shards[0], 2 * hidden + at, quarter).astype(F32)
-
-    @pl.when(step == 0)
-    def _():
+    loads, stores = [], []
+    for kind, (source, stage, target) in enumerate(
+        ((grad_in, grad_stage, grad), (result_in, result_stage, result))
+    ):
+        for w in range(sizes.windows):
+            rows = pl.ds(w * WSLOT, WSLOT)
+            loads.append(pltpu.make_async_copy(source.at[rows, :], stage.at[rows, :], sems.at[0, kind, w]))
+            stores.append(pltpu.make_async_copy(stage.at[rows, :], target.at[rows, :], sems.at[1, kind, w]))
+            loads[-1].start()
+    half = hidden // 2
+
+    def unpack_expand(at):
+        o_we[:width, at : at + half] = total_rows(feed, shards[0], at, half).astype(F32).T
+        o_we[width:, at : at + half] = total_rows(feed, shards[0], hidden + at, half).astype(F32).T
+
+    def unpack_rest():
+        o_ws[...] = total_rows(feed, shards[0], 2 * hidden, hidden).astype(F32)
         for source, shard, base, group in (
-            (early, shards[0], 3 * hidden, (o_cq, o_ck, o_cv, o_cm)), (late, shards[1], 0, (o_sq, o_sk, o_sv, o_sm))
+            (cross, shards[1], 0, (o_cq, o_ck, o_cv, o_cm)), (late, shards[2], 0, (o_sq, o_sk, o_sv, o_sm))
         ):
             for i, ref in enumerate(group):
                 total = total_rows(source, shard, base + i * width, width).astype(F32)
@@ -841,6 +858,15 @@
         for i, ref in enumerate((o_sgain, o_sbias, o_cgain, o_cbias, o_fgain, o_fbias)):
             ref[...] = totals[i : i + 1, :]
 
+    between = [functools.partial(unpack_expand, 0), functools.partial(unpack_expand, half), unpack_rest]
+    for number, (load, store) in enumerate(zip(loads, stores, strict=True)):
+        load.wait()
+        store.start()
+        if number % 2 == 1 and between:
+            between.pop(0)()
+    for store in stores:
+        store.wait()
+
 
 def local(features, cotangent, slot_pair, crop_size, *weights):
     rows, width = features.shape[1:]
@@ -856,7 +882,7 @@
     sizes = types.SimpleNamespace(
         rows=rows, width=width, hidden=hidden, windows=rows // WSLOT, peers=peers,
         scale=1.0 / math.sqrt(2.0 * rows * peers),
-        plans={"early": plan(3 * hidden + 4 * width), "late": plan(4 * width, 16)},
+        plans={"feed": plan(3 * hidden), "cross": plan(4 * width), "late": plan(4 * width, 16)},
     )
     flat = lambda value: value.reshape(1, -1) if value.ndim == 1 else value
     shape = jax.ShapeDtypeStruct
@@ -869,7 +895,7 @@
     middle = pl.pallas_call(
         functools.partial(layer_kernel, sizes),
         in_specs=[small, small, scalar, scalar] + [small] * 16,
-        out_specs=[large] * 4 + [small],
+        out_specs=[large] * 5 + [small],
         out_shape=big + [
             shape((2, plan.owners, plan.kept, width), BF16) for plan in sizes.plans.values()
         ] + [shape((16, width), F32)],
@@ -879,6 +905,10 @@
         ),
         name="layer",
     )(features[0], cotangent[0], slot_pair, crop_size.T, *[flat(weight) for weight in weights])
+    smalls = [
+        square, square, square, square, row, row, square, square, square, square, row, row,
+        shape((2 * width, hidden), F32), shape((hidden, width), F32), row, row,
+    ]
     moved = [pl.BlockSpec((WSLOT, width), lambda w: (w, 0))] * 2
     whole = lambda shape: pl.BlockSpec(shape, lambda w: (0,) * len(shape))
     smalls = [
@@ -887,14 +917,13 @@
     ]
     outs = pl.pallas_call(
         functools.partial(hand_out, sizes),
-        grid=(sizes.windows,),
-        in_specs=moved + [whole(value.shape) for value in middle[2:]],
-        out_specs=moved + [whole(value.shape) for value in smalls[:12]] + [
-            pl.BlockSpec((2 * width, hidden // sizes.windows), lambda w: (0, w)),
-            pl.BlockSpec((hidden // sizes.windows, width), lambda w: (w, 0)),
-            whole(row.shape), whole(row.shape),
+        in_specs=[large, large] + [small] * 4,
+        out_specs=[large, large] + [small] * 16,
+        out_shape=big + smalls,
+        scratch_shapes=[
+            pltpu.VMEM((rows, width), BF16), pltpu.VMEM((rows, width), F32),
+            pltpu.SemaphoreType.DMA((2, 2, sizes.windows)),
         ],
-        out_shape=big + smalls,
         compiler_params=pltpu.CompilerParams(vmem_limit_bytes=60 * 2**20),
         name="hand_out",
     )(*middle)

time: 123 us -> 124 us (level)
  no operation moved by 1% of the time
where the time goes in v3:
time: 124 us
  Pallas kernels  123 us (99%)
  between operations  1.5 us (1%)
    pallas_call x1, Pallas kernels, local(): pl.pallas_call(functools.partial(layer_kernel, sizes), in_specs=[small, s...  117 us
    pallas_call x1, Pallas kernels, local(): pl.pallas_call(functools.partial(hand_out, sizes), in_specs=[large, large...  5.55 us

profile of v3, /device:TPU:0, one launch (start us, length us, event | category | flops | bytes accessed | tf_op | source)
XLA Modules:
  0.0 124.0 jit_solution(11860293407161921747)
XLA Ops:
  1.3 117.0 %layer.1 = (bf16[4608,128]{1,0:T(8,128)(2,1)}, f32[4608,128]{1,0:T(8,128)}, bf16[2,16,96,128]{3,2,1,0:T(8,128)(2,1)}, bf16[2,16,16,128]{3,2,1,0:T(8,128)(2,1)}, ...) custom-call(bf16[4608,128]{1,0:T(8,128)(2,1)} %bitcast.17, bf16[4608,128]{1,0:T(8,128)(2,1)} %bitcast.18, ...), custom_call_target="tpu_custom_call" | custom-call | tf_op jit(solution)/shard_map/layer/pallas_call | solution.py:895
  118.3 5.5 %hand_out.1 = (bf16[4608,128]{1,0:T(8,128)(2,1)}, f32[4608,128]{1,0:T(8,128)}, f32[128,128]{1,0:T(8,128)}, f32[128,128]{1,0:T(8,128)}, f32[128,128]{1,0:T(8,128)...) custom-call(bf16[4608,128]{1,0:T(8,128)(2,1)} %get-tuple-element.42., ...), custom_call_target="tpu_custom_call" | custom-call | tf_op jit(solution)/shard_map/hand_out/pallas_call | solution.py:918

commit v4 on v1

--- a/solution.py
+++ b/solution.py
@@ -19,9 +19,11 @@
 MESH = pl.DeviceIdType.MESH
 TAIL_SHIFT = 2.7777777777777777
 TAIL_POLY = (0.39765776262463953, 1.1594294101832299, 1.9333185594349698, 10.032517622923805, -5.2492700447308085, -9.371923274701059)
-SPAN = 256
+SPAN = 384
 CHUNK = 128
-TILES = ((0, 256), (256, 256), (512, 256), (768, 256), (1024, 128))
+TILES = ((0, 512), (512, 512), (1024, 128))
+WIDE = 512
+BLOCK = 256
 ONES = 16
 
 
@@ -275,15 +277,15 @@
 
     def settle(i, total):
         r.x1[:, span(i)] += total[:width]
-        r.grad_normed[:, span(i)] = total[width:]
-
-    parts = [slice(start, start + SPAN) for start in range(0, hidden, SPAN)]
+        r.grad_normed[:, span(lax.rem(i, per_half))] = total[width:]
+
+    parts = [slice(start, start + BLOCK) for start in range(0, hidden, BLOCK)]
 
     def expand(i):
-        r.buf_a[:hidden, :] = nn(r.expand_t[...], r.concat[:, span(i)])
+        r.buf_a[:hidden, :SPAN] = nn(r.expand_t[...], r.concat[:, span(i)])
 
     def activate(b, rows):
-        act, slope = gelu_both(r.buf_a[rows, :])
+        act, slope = gelu_both(r.buf_a[rows, :SPAN])
         r.act[b, rows, :] = act
         r.slope[b, rows, :] = slope
 
@@ -320,7 +322,8 @@
                 for_shrink = nt(r.act[old], r.branch[old])
                 norm_tile(i, b, branch, up_all, 0)
                 for_expand = nt(r.hid[...], r.concat[:, span(before)])
-                norm_tile(i, b, branch, up_all, CHUNK)
+                for start in range(CHUNK, SPAN, CHUNK):
+                    norm_tile(i, b, branch, up_all, start)
                 r.g_ws[...] += for_shrink
                 r.g_we[...] += for_expand
             return carry
@@ -353,7 +356,7 @@
         dqkv = r.dqkv.at[w]
         upstream(
             w, nn(r.cross_merge_t[...], r.out_two[:, cols_at(w)]),
-            lambda start: r.grad_normed[:, cols_at(w, start, CHUNK)],
+            lambda start: r.grad_normed[:, cols_at(lax.rem(w, 2), start, CHUNK)],
             2, "cgain", r.out_two, r.g_cm, r.cm, r.inverse_two,
         )
         other = r.other[rows_at(w), :]
@@ -639,7 +642,7 @@
         "other": vmem((rows, width), BF16),
         "back": vmem((windows, width, WSLOT), BF16),
         "received": vmem((windows, width, WSLOT), BF16),
-        "grad_normed": vmem((width, rows), F32),
+        "grad_normed": vmem((width, 2 * WSLOT), F32),
         "exps": vmem((windows, WSLOT, WSLOT), BF16),
         "exps_two": vmem((2, WSLOT, WSLOT), BF16),
         "diff": vmem((WSLOT, WSLOT), BF16),
@@ -647,8 +650,8 @@
         "slope": vmem((3, hidden, SPAN), BF16),
         "branch": vmem((3, width, SPAN), BF16),
         "hid": vmem((hidden, SPAN), BF16),
-        "buf_a": vmem((max(WSLOT, hidden), SPAN), F32),
-        "buf_b": vmem((WSLOT, SPAN), F32),
+        "buf_a": vmem((max(WSLOT, hidden), WIDE), F32),
+        "buf_b": vmem((WSLOT, WIDE), F32),
         "grad_merged": vmem((width, WSLOT), BF16),
         "k_t": vmem((width, WSLOT), BF16),
         "v": vmem((WSLOT, width), BF16),
@@ -695,15 +698,25 @@
     result_in, grad_in, early, late, totals, result, grad = refs[:7]
     (o_sq, o_sk, o_sv, o_sm, o_sgain, o_sbias, o_cq, o_ck, o_cv, o_cm, o_cgain, o_cbias,
      o_we, o_ws, o_fgain, o_fbias) = refs[7:23]
+    result_stage, grad_stage, sems = refs[23:]
     width, hidden = sizes.width, sizes.hidden
     shards = [plan.shard for plan in sizes.plans.values()]
-    result[...] = result_in[...]
-    grad[...] = grad_in[...]
-
-    @pl.when(pl.program_id(0) == 0)
-    def _():
-        o_we[:width, :] = total_rows(early, shards[0], 0, hidden).astype(F32).T
-        o_we[width:, :] = total_rows(early, shards[0], hidden, hidden).astype(F32).T
+    loads, stores = [], []
+    for kind, (source, stage, target) in enumerate(
+        ((grad_in, grad_stage, grad), (result_in, result_stage, result))
+    ):
+        for w in range(sizes.windows):
+            rows = pl.ds(w * WSLOT, WSLOT)
+            loads.append(pltpu.make_async_copy(source.at[rows, :], stage.at[rows, :], sems.at[0, kind, w]))
+            stores.append(pltpu.make_async_copy(stage.at[rows, :], target.at[rows, :], sems.at[1, kind, w]))
+            loads[-1].start()
+    half = hidden // 2
+
+    def unpack_expand(at):
+        o_we[:width, at : at + half] = total_rows(early, shards[0], at, half).astype(F32).T
+        o_we[width:, at : at + half] = total_rows(early, shards[0], hidden + at, half).astype(F32).T
+
+    def unpack_rest():
         o_ws[...] = total_rows(early, shards[0], 2 * hidden, hidden).astype(F32)
         for source, shard, base, group in (
             (early, shards[0], 3 * hidden, (o_cq, o_ck, o_cv, o_cm)), (late, shards[1], 0, (o_sq, o_sk, o_sv, o_sm))
@@ -713,6 +726,15 @@
                 ref[...] = total if i == 3 else total.T
         for i, ref in enumerate((o_sgain, o_sbias, o_cgain, o_cbias, o_fgain, o_fbias)):
             ref[...] = totals[i : i + 1, :]
+
+    between = [functools.partial(unpack_expand, 0), functools.partial(unpack_expand, half), unpack_rest]
+    for number, (load, store) in enumerate(zip(loads, stores, strict=True)):
+        load.wait()
+        store.start()
+        if number % 2 == 1 and between:
+            between.pop(0)()
+    for store in stores:
+        store.wait()
 
 
 def local(features, cotangent, slot_pair, crop_size, *weights):
@@ -752,6 +774,10 @@
         ),
         name="layer",
     )(features[0], cotangent[0], slot_pair, crop_size.T, *[flat(weight) for weight in weights])
+    smalls = [
+        square, square, square, square, row, row, square, square, square, square, row, row,
+        shape((2 * width, hidden), F32), shape((hidden, width), F32), row, row,
+    ]
     moved = [pl.BlockSpec((WSLOT, width), lambda w: (w, 0))] * 2
     whole = lambda shape: pl.BlockSpec(shape, lambda w: (0,) * len(shape))
     smalls = [
@@ -760,10 +786,13 @@
     ]
     outs = pl.pallas_call(
         functools.partial(hand_out, sizes),
-        grid=(sizes.windows,),
-        in_specs=moved + [whole(value.shape) for value in middle[2:]],
-        out_specs=moved + [whole(value.shape) for value in smalls],
+        in_specs=[large, large] + [small] * 3,
+        out_specs=[large, large] + [small] * 16,
         out_shape=big + smalls,
+        scratch_shapes=[
+            pltpu.VMEM((rows, width), BF16), pltpu.VMEM((rows, width), F32),
+            pltpu.SemaphoreType.DMA((2, 2, sizes.windows)),
+        ],
         compiler_params=pltpu.CompilerParams(vmem_limit_bytes=60 * 2**20),
         name="hand_out",
     )(*middle)

time: 123 us -> 128 us (1.041)
  Pallas kernels: 121 us -> 127 us
    pallas_call x1, Pallas kernels: 116 us -> 121 us  [local(): pl.pallas_call(functools.partial(layer_kernel, sizes), in_specs=[small, s...]
where the time goes in v4:
time: 128 us
  Pallas kernels  127 us (99%)
  between operations  1.5 us (1%)
    pallas_call x1, Pallas kernels, local(): pl.pallas_call(functools.partial(layer_kernel, sizes), in_specs=[small, s...  121 us
    pallas_call x1, Pallas kernels, local(): pl.pallas_call(functools.partial(hand_out, sizes), in_specs=[large, large...  5.59 us

profile of v4, /device:TPU:0, one launch (start us, length us, event | category | flops | bytes accessed | tf_op | source)
XLA Modules:
  0.0 128.2 jit_solution(10849547582647235649)
XLA Ops:
  1.3 121.1 %layer.1 = (bf16[4608,128]{1,0:T(8,128)(2,1)}, f32[4608,128]{1,0:T(8,128)}, bf16[2,16,112,128]{3,2,1,0:T(8,128)(2,1)}, bf16[2,16,16,128]{3,2,1,0:T(8,128)(2,1)}, f32[16,128]{1,0:T(8,128)}) custom-call(bf16[4608,128]{1,0:T(8,128)(2,1)} %bitcast.17, bf16[4608,128]{1,0:T(8,128)(2,1)} %bitcast.18, s32[1]{0:T(128)S(6)} %copy.38.refs_2_, s32[2,16]{1,0:T(2,128)} %bitcast.19, ...), custom_call_target="tpu_custom_call" | custom-call | tf_op jit(solution)/shard_map/layer/pallas_call | solution.py:764
  122.4 5.6 %hand_out.1 = (bf16[4608,128]{1,0:T(8,128)(2,1)}, f32[4608,128]{1,0:T(8,128)}, f32[128,128]{1,0:T(8,128)}, f32[128,128]{1,0:T(8,128)}, f32[128,128]{1,0:T(8,128)...) custom-call(bf16[4608,128]{1,0:T(8,128)(2,1)} %get-tuple-element.41., ...), custom_call_target="tpu_custom_call" | custom-call | tf_op jit(solution)/shard_map/hand_out/pallas_call | solution.py:787
